TPU v7x, 512 devices: a whole 4x4x16 slice. The times are simulated.
512 devices in a mesh: learner: 32 (over z, y_lo), pool: 4 (over x), tp: 4 (over y_hi, core).
Axes of the slice: x: 4, y: 4 (y_hi: 2, y_lo: 2; y = y_hi * 2 + y_lo), z: 16, core: 2. Of those that a mesh axis runs over, the one named last changes fastest.
Arguments:
- gate_master: float32 [8192, 16384], P('pool', ('learner', 'tp')), may hold values from -0.0625 to 0.0625
- up_master: float32 [8192, 16384], P('pool', ('learner', 'tp')), may hold values from -0.0625 to 0.0625
- stream: float32 [2048, 8192], P(('pool', 'tp'), 'learner'), may hold values from -700 to 700
- norm_gain: float32 [8192], P('learner'), may hold values from 0.1 to 1.9
- live_rows: int32 [2048], P(('pool', 'tp')), may hold values from 0 to 1, as said below
Outputs:
- hidden: bfloat16 [2048, 16384], P('pool', ('learner', 'tp'))
Inputs may be any that keep to these rules, and one draw needn't show every extreme that they name: `live_rows`: within each aligned block of 128 rows (the rows of one device) at most 64 are 1, and some block has exactly 64.
All inputs are finite; a program needn't handle non-finite values.
Results may differ from a plain program's by a relative error of at most 0.009.
Values may be sent and summed in bfloat16 or wider, within the bound.
No kernel may reach another device: no remote copies, remote signals or barrier semaphores. Data moves between devices by JAX's collectives and lax.ppermute only.
A program may use at most 64 MiB of HBM per device.

v0:
```python
import jax
import jax.numpy as jnp
from jax import lax
from jax.sharding import PartitionSpec as P

D = 8192
BLOCK = 32


def block_power(largest):
    power_scale = jnp.full(largest.shape, 2.0 ** (-34), largest.dtype)
    for exponent in range(-32, 5):
        power_scale = jnp.where(largest >= 2.0**exponent, 2.0 ** (exponent - 2), power_scale)
    return power_scale


def snap_grid(ratio):
    magnitude = jnp.abs(ratio)
    level = jnp.zeros_like(ratio)
    for edge, rise in (
        (0.25, 0.5),
        (0.75, 0.5),
        (1.25, 0.5),
        (1.75, 0.5),
        (2.5, 1.0),
        (3.5, 1.0),
        (5.0, 2.0),
    ):
        level = level + jnp.where(magnitude >= edge, rise, 0.0)
    return jnp.sign(ratio) * level


def pack_blocks(master):
    row_total, col_total = master.shape
    grouped = master.reshape(row_total, col_total // BLOCK, BLOCK)
    largest = jnp.max(jnp.abs(grouped), axis=2)
    power_scale = block_power(largest)
    packed = snap_grid(grouped / power_scale[:, :, None]).astype(jnp.bfloat16)
    return (packed.reshape(row_total, col_total), power_scale.astype(jnp.bfloat16))


def unpack_blocks(packed, block_scale):
    row_total, col_total = packed.shape
    grouped = packed.reshape(row_total, col_total // BLOCK, BLOCK).astype(jnp.float32)
    restored = grouped * block_scale[:, :, None].astype(jnp.float32)
    return restored.astype(jnp.bfloat16).reshape(row_total, col_total)


def shards(gate_master, up_master, stream, norm_gain, live_rows):
    gate_packed, gate_scale = pack_blocks(gate_master)
    up_packed, up_scale = pack_blocks(up_master)
    gate_packed, gate_scale, up_packed, up_scale = (
        lax.all_gather(gate_packed, "pool", axis=0, tiled=True),
        lax.all_gather(gate_scale, "pool", axis=0, tiled=True),
        lax.all_gather(up_packed, "pool", axis=0, tiled=True),
        lax.all_gather(up_scale, "pool", axis=0, tiled=True),
    )
    gate_weight = unpack_blocks(gate_packed, gate_scale)
    up_weight = unpack_blocks(up_packed, up_scale)
    square_sum = lax.psum(jnp.sum(stream * stream, axis=1), "learner")
    inverse = lax.rsqrt(square_sum / D + 1e-06)
    normed = (stream * inverse[:, None] * norm_gain[None, :]).astype(jnp.bfloat16)
    live_scale = live_rows.astype(jnp.bfloat16)[:, None]
    gathered = lax.all_gather(normed * live_scale, "tp", axis=0, tiled=True)
    column_piece = lax.all_gather(gathered, "learner", axis=1, tiled=True)
    gate_sum = jnp.dot(column_piece, gate_weight, preferred_element_type=jnp.float32)
    up_sum = jnp.dot(column_piece, up_weight, preferred_element_type=jnp.float32)
    return (jax.nn.silu(gate_sum) * up_sum).astype(jnp.bfloat16)


def solution(mesh):
    placed = (
        P("pool", ("learner", "tp")),
        P("pool", ("learner", "tp")),
        P(("pool", "tp"), "learner"),
        P("learner"),
        P(("pool", "tp")),
    )
    return jax.shard_map(
        shards, mesh=mesh, in_specs=placed, out_specs=P("pool", ("learner", "tp")), check_vma=False
    )
```

profile of v0, /device:TPU:28, one launch (start us, length us, event | category | flops | bytes accessed | tf_op | source)
XLA Modules:
  0.0 359.4 jit_solution(9469155296797741874)
XLA Ops:
  6.5 1.6 copy.7
  8.1 0.1 bitcast_reduce_fusion.1
  8.2 0.2 fusion.4
  8.4 1.9 multiply_convert_fusion.1
  10.3 0.0 all-gather.8.cloned.1.call-start
  10.4 0.3 copy.9
  10.7 0.1 bitcast_reduce_fusion
  10.9 0.2 fusion.5
  11.0 1.9 multiply_convert_fusion
  12.9 0.0 all-gather.4.cloned.1.call-start
  13.0 0.1 multiply_reduce_fusion
  13.1 67.6 %psum.7 = f32[128]{0:T(128)S(1)} all-reduce(f32[128]{0:T(128)S(1)} %multiply_reduce_fusion), channel_id=1, replica_groups=mesh['learner'=32,'pool'=4,'tp'=4] {'learner'}, use_global_device_ids=true, to_apply=%region_1.2 | all-reduce | flops 128 | bytes 1024 | tf_op jit(solution)/shard_map/psum | solution.py:60
  80.7 0.1 fusion.3
  80.8 7.7 %all_gather.18 = bf16[512,256]{1,0:T(8,128)(2,1)} all-gather(bf16[128,256]{1,0:T(8,128)(2,1)S(1)} %fusion.3), channel_id=1, replica_groups=mesh['learner'=32,'pool'=4,'tp'=4] {'tp'}, dimensions={0}, use_global_device_ids=true | all-gather | bytes 327680 | tf_op jit(solution)/shard_map/all_gather | solution.py:64
  88.5 10.7 %all_gather.21 = bf16[8192,4]{0,1:T(4,128)(2,1)S(1)} all-gather(bf16[2048,4]{0,1:T(4,128)(2,1)S(1)} %get-tuple-element.5), channel_id=1, replica_groups=mesh['learner'=32,'pool'=4,'tp'=4] {'pool'}, dimensions={0}, use_global_device_ids=true | all-gather | bytes 81920 | tf_op jit(solution)/shard_map/all_gather | solution.py:54
  99.2 11.9 %all_gather.23 = bf16[8192,4]{0,1:T(4,128)(2,1)S(1)} all-gather(bf16[2048,4]{0,1:T(4,128)(2,1)S(1)} %get-tuple-element.7), channel_id=1, replica_groups=mesh['learner'=32,'pool'=4,'tp'=4] {'pool'}, dimensions={0}, use_global_device_ids=true | all-gather | bytes 81920 | tf_op jit(solution)/shard_map/all_gather | solution.py:56
  111.1 0.0 all-gather.6.cloned.1.call-done
  111.1 2.0 fusion.1
  113.2 0.0 all-gather.8.cloned.1.call-done
  113.2 3.3 fusion
  116.5 226.9 %all-gather.4.cloned.1.call-done = bf16[512,8192]{1,0:T(8,128)(2,1)} async-done(((bf16[512,256]{1,0:T(8,128)(2,1)}), bf16[512,8192]{1,0:T(8,128)(2,1)}) %all-gather.4.cloned.1.call-update) | async-done | bytes 8388624 | tf_op jit(solution)/shard_map/all_gather | solution.py:65
  343.4 5.9 %fusion.6 = f32[512,128]{1,0:T(8,128)S(1)} fusion(bf16[512,8192]{1,0:T(8,128)(2,1)} %all-gather.4.cloned.1.call-done, bf16[8192,128]{0,1:T(8,128)(2,1)S(1)} %fusion.1), kind=kOutput, calls=%fused_computation.30 | convolution fusion | flops 1073741824 | bytes 10747904 | tf_op jit(solution)/shard_map/dot_general | solution.py:66
  349.3 0.5 copy-done.4
  349.8 3.0 fusion.2
  (19 shorter events, 0.1 us)
Async XLA Ops:
  6.5 104.6 %all-gather.6.cloned.1.call-start = ((), (), s32[]{:S(2)}) async-start(), calls=%async_computation.1 | async-start | bytes 2621440 | tf_op jit(solution)/shard_map/all_gather | solution.py:53
  8.1 2.2 copy-start.1
  10.3 102.9 %all-gather.8.cloned.1.call-start = ((), (), s32[]{:S(2)}) async-start(), calls=%async_computation.2 | async-start | bytes 2621440 | tf_op jit(solution)/shard_map/all_gather | solution.py:55
  10.7 2.3 copy-start.5
  10.7 2.3 copy-start.2
  10.7 70.0 %copy-start.3 = (f32[256]{0:T(256)S(1)}, f32[256]{0:T(256)}, u32[]{:S(2)}) copy-start(f32[256]{0:T(256)} %param.8) | copy-start | bytes 3076
  12.9 330.5 %all-gather.4.cloned.1.call-start = ((), (), s32[]{:S(2)}) async-start(), calls=%async_computation | async-start | bytes 8650752 | tf_op jit(solution)/shard_map/all_gather | solution.py:65
  343.4 5.9 %copy-start = (bf16[8192,128]{0,1:T(8,128)(2,1)S(1)}, bf16[8192,128]{0,1:T(8,128)(2,1)}, u32[]{:S(2)}) copy-start(bf16[8192,128]{0,1:T(8,128)(2,1)} %fusion) | copy-start | bytes 6291460
  343.4 6.4 %copy-start.4 = (bf16[512,8192]{1,0:T(8,128)(2,1)S(1)}, bf16[512,8192]{1,0:T(8,128)(2,1)}, u32[]{:S(2)}) copy-start(bf16[512,8192]{1,0:T(8,128)(2,1)} %all-gather.4.cloned.1.call-done) | copy-start | bytes 25165828
Sparse Core Ops, SparseCore 0:
  10.4 41.4 all-gather.5
  54.0 38.6 all-gather.7
  94.7 248.6 all-gather.3
where the time goes:
time: 360 us; the launch traced here: 359 us
  waiting for transfers between devices  227 us (63%)
  blocking collectives  97.8 us (27%)
  between operations  13.3 us (4%)
  other arithmetic  9.92 us (3%)
  matrix products  8.85 us (2%)
    all_gather x1, waiting for transfers between devices, shards(): column_piece = lax.all_gather(gathered, 'learner', axis=1, tiled=True)  227 us
    psum x1, blocking collectives, shards(): square_sum = lax.psum(jnp.sum(stream * stream, axis=1), 'learner')  67.6 us
    all_gather x1, blocking collectives, shards(): lax.all_gather(up_scale, 'pool', axis=0, tiled=True)  11.9 us
    all_gather x1, blocking collectives, shards(): lax.all_gather(gate_scale, 'pool', axis=0, tiled=True)  10.7 us
    all_gather x1, blocking collectives, shards(): gathered = lax.all_gather(normed * live_scale, 'tp', axis=0, tiled=True)  7.74 us
  transfers between devices with their start and end apart: 3, of which 1 were waited for; matrix products, arithmetic and copies ran while one was open for 2% of the time, Pallas kernels for 0%

commit v1 on v0

v1 whole, which is shorter than its diff:
```python
import jax
import jax.numpy as jnp
from jax import lax
from jax.experimental import pallas as pl
from jax.experimental.pallas import tpu as pltpu
from jax.sharding import Mesh, PartitionSpec as P

D = 8192
LIVE = 64
ROWS = 128
FEATS = 256
EXTRA = 16
BLOCK_ROWS = LIVE + EXTRA
CHUNK_ROWS = 2 * LIVE + EXTRA
AXES = ("zh", "zl", "yl", "x", "yh", "c")
BF = jnp.bfloat16
F32 = jnp.float32
VMEM_BYTES = 48 * 1024 * 1024


def split3(value):
    hi = value.astype(BF).astype(F32)
    mid = (value - hi).astype(BF).astype(F32)
    lo = (value - hi - mid).astype(BF).astype(F32)
    return hi, mid, lo


def diagonal(size):
    return lax.broadcasted_iota(jnp.int32, (size, size), 0) == lax.broadcasted_iota(jnp.int32, (size, size), 1)


def slot_table(live):
    rows = lax.broadcasted_iota(jnp.int32, (ROWS, ROWS), 0)
    cols = lax.broadcasted_iota(jnp.int32, (ROWS, ROWS), 1)
    before = jnp.where(rows <= cols, 1.0, 0.0).astype(BF)
    wide = jnp.broadcast_to(live, (16, ROWS))
    rank = jnp.dot(wide.astype(BF), before, preferred_element_type=F32)[0:1, :]
    slot = lax.broadcasted_iota(jnp.int32, (LIVE, ROWS), 0).astype(F32) + 1.0
    return jnp.where((slot == rank) & (live > 0.5), 1.0, 0.0)


def compact_kernel(stream_ref, gain_ref, live_ref, out_ref):
    stream = stream_ref[...]
    live = live_ref[...].astype(F32)
    table = slot_table(live)
    scaled = (stream * gain_ref[...]).astype(BF)
    rows = jnp.dot(table.astype(BF), scaled, preferred_element_type=F32)
    out_ref[0:LIVE, :] = rows.astype(BF)
    square = jnp.sum(stream * stream, axis=1, keepdims=True)
    square_row = jnp.sum(jnp.where(diagonal(ROWS), square, 0.0), axis=0, keepdims=True)
    hi, mid, lo = split3(square_row)
    index = lax.broadcasted_iota(jnp.int32, (EXTRA, ROWS), 0)
    out_ref[LIVE:, 0:ROWS] = jnp.where(index == 0, live, jnp.where(index == 1, mid, 0.0)).astype(BF)
    out_ref[LIVE:, ROWS:] = jnp.where(index == 0, hi, jnp.where(index == 1, lo, 0.0)).astype(BF)


def compact(stream, gain, live):
    return pl.pallas_call(
        compact_kernel,
        out_shape=jax.ShapeDtypeStruct((BLOCK_ROWS, FEATS), BF),
        name="compact",
    )(stream, gain.reshape(1, FEATS), live.reshape(1, ROWS))


def restore(master):
    tile = master.T.reshape(4, 32, 128)
    size = jnp.abs(tile)
    largest = jnp.max(size, axis=1, keepdims=True)
    wide = largest * 8388609.0
    power = jnp.abs(wide - wide * (1.0 - 2.0**-24))
    power = jnp.where(power > largest, power * 0.5, power)
    power = jnp.where(power * 2.0 <= largest, power * 2.0, power)
    scale = jnp.clip(power, 2.0**-32, 2.0**4) * 0.25
    level = jnp.zeros_like(size)
    for edge, value in ((0.25, 0.5), (0.75, 1.0), (1.25, 1.5), (1.75, 2.0), (2.5, 3.0), (3.5, 4.0), (5.0, 6.0)):
        level = jnp.where(size >= scale * edge, scale * value, level)
    return jnp.where(tile < 0.0, -level, level).reshape(128, 128).T.astype(BF)


def pack_kernel(yl_ref, gate_ref, up_ref, same_ref, flip_ref):
    yl = yl_ref[0]
    for out_ref, half in ((same_ref, yl), (flip_ref, 1 - yl)):
        for tile in range(2):
            rows = pl.ds(pl.multiple_of(half * FEATS + tile * 128, 128), 128)
            out_ref[0, tile * 128 : (tile + 1) * 128, 0:128] = restore(gate_ref[rows, :])
            out_ref[0, tile * 128 : (tile + 1) * 128, 128:256] = restore(up_ref[rows, :])


def pack(yl, gate_master, up_master):
    shape = jax.ShapeDtypeStruct((4, FEATS, 256), BF)
    return pl.pallas_call(
        pack_kernel,
        grid=(4,),
        in_specs=[
            pl.BlockSpec(memory_space=pltpu.SMEM),
            pl.BlockSpec((2 * FEATS, 128), lambda i: (i, 0)),
            pl.BlockSpec((2 * FEATS, 128), lambda i: (i, 0)),
        ],
        out_specs=[pl.BlockSpec((1, FEATS, 256), lambda i: (i, 0, 0))] * 2,
        out_shape=[shape, shape],
        compiler_params=pltpu.CompilerParams(vmem_limit_bytes=VMEM_BYTES),
        name="pack",
    )(yl, gate_master, up_master)


def partial_kernel(y_ref, own_ref, other_ref, w00_ref, w01_ref, w10_ref, w11_ref, out_ref):
    yl, yh = y_ref[0], y_ref[1]
    index = lax.broadcasted_iota(jnp.int32, (EXTRA, ROWS), 0)
    left = [jnp.zeros((EXTRA, ROWS), F32) for _ in range(4)]
    right = [jnp.zeros((EXTRA, ROWS), F32) for _ in range(4)]
    for part, a_ref in enumerate((own_ref, other_ref)):
        for pool in range(4):
            square = jnp.zeros((1, ROWS), F32)
            for block in range(4):
                tail = a_ref[pool, block, LIVE:, :].astype(F32)
                square = square + tail[0:1, ROWS:] + tail[1:2, :ROWS] + tail[1:2, ROWS:]
            live = a_ref[pool, 0, LIVE:, :].astype(F32)[0:1, :ROWS]
            hi, mid, lo = split3(square)
            top, low = index == 2 * part, index == 2 * part + 1
            left[pool] = jnp.where(top, live, jnp.where(low, mid, left[pool]))
            right[pool] = jnp.where(top, hi, jnp.where(low, lo, right[pool]))
    for flip_l, flip_h, w_ref in ((0, 0, w00_ref), (0, 1, w01_ref), (1, 0, w10_ref), (1, 1, w11_ref)):
        to_l, to_h = lax.rem(yl + flip_l, 2), lax.rem(yh + flip_h, 2)
        for part, a_ref in enumerate((own_ref, other_ref)):
            total = jnp.zeros((4 * LIVE, 256), F32)
            for block in range(4):
                rows = a_ref[:, block, 0:LIVE, :].reshape(4 * LIVE, FEATS)
                total = total + jnp.dot(rows, w_ref[block], preferred_element_type=F32)
            for pool in range(4):
                out_ref[to_l, pool, to_h, part * LIVE : (part + 1) * LIVE, :] = total[
                    pool * LIVE : (pool + 1) * LIVE, :
                ].astype(BF)
        for pool in range(4):
            out_ref[to_l, pool, to_h, 2 * LIVE :, 0:ROWS] = left[pool].astype(BF)
            out_ref[to_l, pool, to_h, 2 * LIVE :, ROWS:] = right[pool].astype(BF)


def partial(place, own, other, weights):
    return pl.pallas_call(
        partial_kernel,
        in_specs=[pl.BlockSpec(memory_space=pltpu.SMEM)] + [pl.BlockSpec(memory_space=pltpu.VMEM)] * 6,
        out_specs=pl.BlockSpec(memory_space=pltpu.VMEM),
        out_shape=jax.ShapeDtypeStruct((2, 4, 2, CHUNK_ROWS, 256), BF),
        compiler_params=pltpu.CompilerParams(vmem_limit_bytes=VMEM_BYTES),
        name="partial",
    )(place, own, other, *weights)


def finish_kernel(c_ref, in_ref, out_ref):
    c = c_ref[0]
    for yh in range(2):
        total = jnp.zeros((2 * LIVE, 256), F32)
        square = [jnp.zeros((1, ROWS), F32) for _ in range(2)]
        for yl in range(2):
            for pool in range(4):
                total = total + in_ref[yl, pool, yh, 0 : 2 * LIVE, :].astype(F32)
                tail = in_ref[yl, pool, yh, 2 * LIVE :, :].astype(F32)
                for part in range(2):
                    top, low = 2 * part, 2 * part + 1
                    square[part] = (
                        square[part] + tail[top : top + 1, ROWS:] + tail[low : low + 1, :ROWS] + tail[low : low + 1, ROWS:]
                    )
        tail = in_ref[0, 0, yh, 2 * LIVE :, :].astype(F32)
        for part in range(2):
            table = slot_table(tail[2 * part : 2 * part + 1, :ROWS])
            inverse = lax.rsqrt(square[part] * (1.0 / D) + 1e-06)
            inverse = jnp.sum(table * inverse, axis=1, keepdims=True)
            rows = total[part * LIVE : (part + 1) * LIVE, :] * inverse
            gate, up = rows[:, :128], rows[:, 128:]
            hidden = (gate / (1.0 + jnp.exp(-gate)) * up).astype(BF)
            spread = lax.dot_general(table.astype(BF), hidden, (((0,), (0,)), ((), ())), preferred_element_type=F32)
            block = 2 * yh + lax.rem(c + part, 2)
            out_ref[pl.ds(pl.multiple_of(block * ROWS, ROWS), ROWS), :] = spread.astype(BF)


def finish(c, received):
    return pl.pallas_call(
        finish_kernel,
        in_specs=[pl.BlockSpec(memory_space=pltpu.SMEM), pl.BlockSpec(memory_space=pltpu.VMEM)],
        out_specs=pl.BlockSpec(memory_space=pltpu.VMEM),
        out_shape=jax.ShapeDtypeStruct((4 * ROWS, 128), BF),
        compiler_params=pltpu.CompilerParams(vmem_limit_bytes=VMEM_BYTES),
        name="finish",
    )(c, received)


def shards(gate_master, up_master, stream, norm_gain, live_rows):
    yl = lax.axis_index("yl")
    place = jnp.stack([yl, lax.axis_index("yh")]).astype(jnp.int32)
    core = lax.axis_index("c").astype(jnp.int32).reshape(1)
    block = compact(stream, norm_gain, live_rows)
    swap = [(zh * 4 + x, x * 4 + zh) for zh in range(4) for x in range(4)]
    block = lax.ppermute(block, ("zh", "x"), swap)
    same, flip = pack(yl.astype(jnp.int32).reshape(1), gate_master, up_master)
    block, same, flip = lax.optimization_barrier((block, same, flip))
    w01 = lax.ppermute(same, "yh", [(0, 1), (1, 0)])
    w10 = lax.ppermute(flip, "yl", [(0, 1), (1, 0)])
    w11 = lax.ppermute(flip, ("yl", "yh"), [(0, 3), (1, 2), (2, 1), (3, 0)])
    own = lax.all_gather(block, ("zh", "zl"), axis=0, tiled=False).reshape(4, 4, BLOCK_ROWS, FEATS)
    own, w01, w10, w11 = lax.optimization_barrier((own, w01, w10, w11))
    other = lax.ppermute(own, "c", [(0, 1), (1, 0)])
    sums = partial(place, own, other, (same, w01, w10, w11))
    sums = sums.reshape(16, CHUNK_ROWS, 256)
    received = lax.all_to_all(sums, ("yl", "x", "yh"), 0, 0)
    return finish(core, received.reshape(2, 4, 2, CHUNK_ROWS, 256))


def solution(mesh):
    fine = Mesh(mesh.devices.reshape(4, 4, 2, 4, 2, 2), AXES)
    learner, tp = ("zh", "zl", "yl"), ("yh", "c")
    placed = (
        P("x", learner + tp),
        P("x", learner + tp),
        P(("x",) + tp, learner),
        P(learner),
        P(("x",) + tp),
    )
    return jax.shard_map(shards, mesh=fine, in_specs=placed, out_specs=P("x", learner + tp), check_vma=False)
```

time: 360 us -> 103 us (0.29)
  the two profiles are of different devices: /device:TPU:28 before, /device:TPU:1 now
where the time goes in v1:
time: 103 us
  blocking collectives  42.1 us (41%)
  starting transfers between devices  28.1 us (27%)
  waiting for transfers between devices  20.7 us (20%)
  Pallas kernels  9.08 us (9%)
  local copies, waits for them, and re-layouts  2.45 us (2%)
    all_gather x1, blocking collectives, shards(): lax.all_gather(block, ('zh', 'zl'), axis=0, tiled=False)  42.1 us
    all_to_all x1, waiting for transfers between devices, shards(): received = lax.all_to_all(sums, ('yl', 'x', 'yh'), 0, 0)  19 us
    ppermute x1, starting transfers between devices, shards(): other = lax.ppermute(own, 'c', [(0, 1), (1, 0)])  9.64 us
    all_to_all x1, starting transfers between devices, shards(): received = lax.all_to_all(sums, ('yl', 'x', 'yh'), 0, 0)  6.78 us
    ppermute x1, starting transfers between devices, shards(): w01 = lax.ppermute(same, 'yh', [(0, 1), (1, 0)])  5.65 us
    pallas_call x1, Pallas kernels, partial(): pl.pallas_call(partial_kernel, in_specs=[pl.BlockSpec(memory_space=pltpu....  2.81 us
    pallas_call x1, Pallas kernels, pack(): pl.pallas_call(pack_kernel, grid=(4,), in_specs=[pl.BlockSpec(memory_spac...  2.72 us
    ppermute x1, starting transfers between devices, shards(): w11 = lax.ppermute(flip, ('yl', 'yh'), [(0, 3), (1, 2), (2, 1), (3, 0)])  2.68 us
  transfers between devices with their start and end apart: 6, of which 2 were waited for; matrix products, arithmetic and copies ran while one was open for 0% of the time, Pallas kernels for 3%

profile of v1, /device:TPU:1, one launch (start us, length us, event | category | flops | bytes accessed | tf_op | source)
XLA Modules:
  0.0 102.5 jit_solution(12735003782217721966)
XLA Ops:
  0.0 1.8 %compact.1 = bf16[80,256]{1,0:T(8,128)(2,1)} custom-call(f32[128,256]{1,0:T(8,128)} %stream_ref.1, f32[1,256]{1,0:T(1,128)} %bitcast.11, s32[1,128]{1,0:T(1,128)} %bitcast.12), custom_call_target="tpu_custom_call" | custom-call | tf_op jit(solution)/shard_map/compact/pallas_call | solution.py:58
  1.8 1.4 %collective-permute-start = (bf16[80,256]{1,0:T(8,128)(2,1)}, bf16[80,256]{1,0:T(8,128)(2,1)S(1)}, u32[]{:S(2)}, u32[]{:S(2)}) collective-permute-start(bf16[80,256]{1,0:T(8,128)(2,1)} %compact.1), channel_id=1, source_target_pairs={{0,0},{4,128},{8,256},{12,384},{128,4},{132,132},{136,260},{140,38... | collective-permute-start | bytes 122888 | tf_op jit(solution)/shard_map/ppermute | solution.py:193
  3.2 0.0 copy-start
  3.2 1.2 %copy-done = f32[2048,128]{1,0:T(8,128)S(1)} copy-done((f32[2048,128]{1,0:T(8,128)S(1)}, f32[2048,128]{1,0:T(8,128)}, u32[]{:S(2)}) %copy-start) | copy-done | bytes 1048600
  4.5 0.0 copy-start.1
  4.5 1.2 %copy-done.1 = f32[2048,128]{1,0:T(8,128)S(1)} copy-done((f32[2048,128]{1,0:T(8,128)S(1)}, f32[2048,128]{1,0:T(8,128)}, u32[]{:S(2)}) %copy-start.1) | copy-done | bytes 1048600
  5.7 2.7 %pack.1 = (bf16[4,256,256]{2,1,0:T(8,128)(2,1)S(1)}, bf16[4,256,256]{2,1,0:T(8,128)(2,1)S(1)}) custom-call(s32[1]{0:T(128)} %bitcast.1.yl_ref, f32[2048,128]{1,0:T(8,128)S(1)} %copy-done, f32[2048,128]{1,0:T(8,128)S(1)} %copy-done.1), custom_call_target="tpu_custom_call" | custom-call | tf_op jit(solution)/shard_map/pack/pallas_call | solution.py:91
  8.4 0.0 collective-permute-done
  8.4 5.7 %collective-permute-start.1 = (bf16[4,256,256]{2,1,0:T(8,128)(2,1)S(1)}, bf16[4,256,256]{2,1,0:T(8,128)(2,1)S(1)}, u32[]{:S(2)}, u32[]{:S(2)}) collective-permute-start(bf16[4,256,256]{2,1,0:T(8,128)(2,1)S(1)} %get-tuple-element.17.w00_ref), channel_id=1, source_target_pairs={{0,2},{2,0},{1,3},{3,1},{4,6},{6,4},{5,7},{7,5},{8,10},{10,8},{9,1... | collective-permute-start | bytes 1572872 | tf_op jit(solution)/shard_map/ppermute | solution.py:196
  14.1 2.7 %collective-permute-start.3 = (bf16[4,256,256]{2,1,0:T(8,128)(2,1)S(1)}, bf16[4,256,256]{2,1,0:T(8,128)(2,1)S(1)}, u32[]{:S(2)}, u32[]{:S(2)}) collective-permute-start(bf16[4,256,256]{2,1,0:T(8,128)(2,1)S(1)} %get-tuple-element.18), channel_id=1, source_target_pairs={{0,18},{2,16},{16,2},{18,0},{1,19},{3,17},{17,3},{19,1},{4,22},{6,... | collective-permute-start | bytes 1572872 | tf_op jit(solution)/shard_map/ppermute | solution.py:198
  16.8 1.9 %collective-permute-start.2 = (bf16[4,256,256]{2,1,0:T(8,128)(2,1)S(1)}, bf16[4,256,256]{2,1,0:T(8,128)(2,1)S(1)}, u32[]{:S(2)}, u32[]{:S(2)}) collective-permute-start(bf16[4,256,256]{2,1,0:T(8,128)(2,1)S(1)} %get-tuple-element.18), channel_id=1, source_target_pairs={{0,16},{16,0},{1,17},{17,1},{2,18},{18,2},{3,19},{19,3},{4,20},{20... | collective-permute-start | bytes 1572872 | tf_op jit(solution)/shard_map/ppermute | solution.py:197
  18.7 42.1 %all-gather = bf16[1280,256]{1,0:T(8,128)(2,1)S(1)} all-gather(bf16[80,256]{1,0:T(8,128)(2,1)S(1)} %collective-permute-done), channel_id=2, replica_groups=mesh['zh'=4,'zl'=4,'yl'=2,'x'=4,'yh'=2,'c'=2] {'zh','zl'}, dimensions={0}, use_global_device_ids=true | all-gather | bytes 696320 | tf_op jit(solution)/shard_map/all_gather | solution.py:199
  60.7 0.0 collective-permute-done.1.w01_ref
  60.7 0.0 collective-permute-done.3.w11_ref
  60.8 0.0 collective-permute-done.2.w10_ref
  60.8 9.6 %collective-permute-start.4 = (bf16[4,4,80,256]{3,2,1,0:T(8,128)(2,1)S(1)}, bf16[4,4,80,256]{3,2,1,0:T(8,128)(2,1)S(1)}, u32[]{:S(2)}, u32[]{:S(2)}) collective-permute-start(bf16[4,4,80,256]{3,2,1,0:T(8,128)(2,1)S(1)} %bitcast.9), channel_id=1, source_target_pairs={{0,1},{1,0},{2,3},{3,2},{4,5},{5,4},{6,7},{7,6},{8,9},{9,8},{10,11... | collective-permute-start | bytes 1966088 | tf_op jit(solution)/shard_map/ppermute | solution.py:201
  70.4 0.1 pad_add_fusion.y_ref
  70.5 1.6 %collective-permute-done.4.other_ref = bf16[4,4,80,256]{3,2,1,0:T(8,128)(2,1)S(1)} collective-permute-done((bf16[4,4,80,256]{3,2,1,0:T(8,128)(2,1)S(1)}, bf16[4,4,80,256]{3,2,1,0:T(8,128)(2,1)S(1)}, u32[]{:S(2)}, u32[]{:S(2)}) %collective-permute-start.4) | collective-permute-done | bytes 655392 | tf_op jit(solution)/shard_map/ppermute | solution.py:201
  72.1 2.8 %partial.1 = bf16[2,4,2,144,256]{4,3,2,1,0:T(8,128)(2,1)} custom-call(s32[2]{0:T(128)S(1)} %pad_add_fusion.y_ref, bf16[4,4,80,256]{3,2,1,0:T(8,128)(2,1)S(1)} %bitcast.10, bf16[4,4,80,256]{3,2,1,0:T(8,128)(2,1)S(1)} %collective-permute-done.4.other_ref, bf16[4,256,256]{2,1,0:T(8,128)(2,1)S(1)} %get-tuple-element.17.w00_ref, ...), custom_call_target="tpu_custom_call" | custom-call | tf_op jit(solution)/shard_map/partial/pallas_call | solution.py:139
  74.9 6.8 %all-to-all-start = ((bf16[16,144,256]{2,1,0:T(8,128)(2,1)}), bf16[16,144,256]{2,1,0:T(8,128)(2,1)S(1)}, u32[]{:S(2)}, u32[]{:S(2)}) async-start(bf16[16,144,256]{2,1,0:T(8,128)(2,1)} %bitcast.6), calls=%async_computation | async-start | bytes 2359296 | tf_op jit(solution)/shard_map/all_to_all | solution.py:204
  81.7 19.0 %all-to-all-done = bf16[16,144,256]{2,1,0:T(8,128)(2,1)S(1)} async-done(((bf16[16,144,256]{2,1,0:T(8,128)(2,1)}), bf16[16,144,256]{2,1,0:T(8,128)(2,1)S(1)}, u32[]{:S(2)}, u32[]{:S(2)}) %all-to-all-start) | async-done | bytes 1179680 | tf_op jit(solution)/shard_map/all_to_all | solution.py:204
  100.8 1.8 %finish.1 = bf16[512,128]{1,0:T(8,128)(2,1)} custom-call(s32[1]{0:T(128)} %bitcast.c_ref, bf16[2,4,2,144,256]{4,3,2,1,0:T(8,128)(2,1)S(1)} %bitcast.8), custom_call_target="tpu_custom_call" | custom-call | tf_op jit(solution)/shard_map/finish/pallas_call | solution.py:177
Async XLA Ops:
  1.8 6.6 %collective-permute-start = (bf16[80,256]{1,0:T(8,128)(2,1)}, bf16[80,256]{1,0:T(8,128)(2,1)S(1)}, u32[]{:S(2)}, u32[]{:S(2)}) collective-permute-start(bf16[80,256]{1,0:T(8,128)(2,1)} %compact.1), channel_id=1, source_target_pairs={{0,0},{4,128},{8,256},{12,384},{128,4},{132,132},{136,260},{140,38... | collective-permute-start | bytes 122888 | tf_op jit(solution)/shard_map/ppermute | solution.py:193
  3.2 1.2 %copy-start = (f32[2048,128]{1,0:T(8,128)S(1)}, f32[2048,128]{1,0:T(8,128)}, u32[]{:S(2)}) copy-start(f32[2048,128]{1,0:T(8,128)} %gate_ref.1) | copy-start | bytes 3145732
  4.5 1.2 %copy-start.1 = (f32[2048,128]{1,0:T(8,128)S(1)}, f32[2048,128]{1,0:T(8,128)}, u32[]{:S(2)}) copy-start(f32[2048,128]{1,0:T(8,128)} %up_ref.1) | copy-start | bytes 3145732
  8.4 52.3 %collective-permute-start.1 = (bf16[4,256,256]{2,1,0:T(8,128)(2,1)S(1)}, bf16[4,256,256]{2,1,0:T(8,128)(2,1)S(1)}, u32[]{:S(2)}, u32[]{:S(2)}) collective-permute-start(bf16[4,256,256]{2,1,0:T(8,128)(2,1)S(1)} %get-tuple-element.17.w00_ref), channel_id=1, source_target_pairs={{0,2},{2,0},{1,3},{3,1},{4,6},{6,4},{5,7},{7,5},{8,10},{10,8},{9,1... | collective-permute-start | bytes 1572872 | tf_op jit(solution)/shard_map/ppermute | solution.py:196
  14.1 46.7 %collective-permute-start.3 = (bf16[4,256,256]{2,1,0:T(8,128)(2,1)S(1)}, bf16[4,256,256]{2,1,0:T(8,128)(2,1)S(1)}, u32[]{:S(2)}, u32[]{:S(2)}) collective-permute-start(bf16[4,256,256]{2,1,0:T(8,128)(2,1)S(1)} %get-tuple-element.18), channel_id=1, source_target_pairs={{0,18},{2,16},{16,2},{18,0},{1,19},{3,17},{17,3},{19,1},{4,22},{6,... | collective-permute-start | bytes 1572872 | tf_op jit(solution)/shard_map/ppermute | solution.py:198
  16.8 44.0 %collective-permute-start.2 = (bf16[4,256,256]{2,1,0:T(8,128)(2,1)S(1)}, bf16[4,256,256]{2,1,0:T(8,128)(2,1)S(1)}, u32[]{:S(2)}, u32[]{:S(2)}) collective-permute-start(bf16[4,256,256]{2,1,0:T(8,128)(2,1)S(1)} %get-tuple-element.18), channel_id=1, source_target_pairs={{0,16},{16,0},{1,17},{17,1},{2,18},{18,2},{3,19},{19,3},{4,20},{20... | collective-permute-start | bytes 1572872 | tf_op jit(solution)/shard_map/ppermute | solution.py:197
  60.8 11.4 %collective-permute-start.4 = (bf16[4,4,80,256]{3,2,1,0:T(8,128)(2,1)S(1)}, bf16[4,4,80,256]{3,2,1,0:T(8,128)(2,1)S(1)}, u32[]{:S(2)}, u32[]{:S(2)}) collective-permute-start(bf16[4,4,80,256]{3,2,1,0:T(8,128)(2,1)S(1)} %bitcast.9), channel_id=1, source_target_pairs={{0,1},{1,0},{2,3},{3,2},{4,5},{5,4},{6,7},{7,6},{8,9},{9,8},{10,11... | collective-permute-start | bytes 1966088 | tf_op jit(solution)/shard_map/ppermute | solution.py:201
  74.9 25.8 %all-to-all-start = ((bf16[16,144,256]{2,1,0:T(8,128)(2,1)}), bf16[16,144,256]{2,1,0:T(8,128)(2,1)S(1)}, u32[]{:S(2)}, u32[]{:S(2)}) async-start(bf16[16,144,256]{2,1,0:T(8,128)(2,1)} %bitcast.6), calls=%async_computation | async-start | bytes 2359296 | tf_op jit(solution)/shard_map/all_to_all | solution.py:204

commit v2 on v1

--- a/solution.py
+++ b/solution.py
@@ -9,7 +9,7 @@
 LIVE = 64
 ROWS = 128
 FEATS = 256
-EXTRA = 16
+EXTRA = 8
 BLOCK_ROWS = LIVE + EXTRA
 CHUNK_ROWS = 2 * LIVE + EXTRA
 AXES = ("zh", "zl", "yl", "x", "yh", "c")
@@ -77,73 +77,79 @@
     return jnp.where(tile < 0.0, -level, level).reshape(128, 128).T.astype(BF)
 
 
-def pack_kernel(yl_ref, gate_ref, up_ref, same_ref, flip_ref):
-    yl = yl_ref[0]
-    for out_ref, half in ((same_ref, yl), (flip_ref, 1 - yl)):
+def pack_kernel(gate_ref, up_ref, out_ref):
+    for half in range(2):
         for tile in range(2):
-            rows = pl.ds(pl.multiple_of(half * FEATS + tile * 128, 128), 128)
-            out_ref[0, tile * 128 : (tile + 1) * 128, 0:128] = restore(gate_ref[rows, :])
-            out_ref[0, tile * 128 : (tile + 1) * 128, 128:256] = restore(up_ref[rows, :])
-
-
-def pack(yl, gate_master, up_master):
-    shape = jax.ShapeDtypeStruct((4, FEATS, 256), BF)
+            rows = slice(half * FEATS + tile * 128, half * FEATS + (tile + 1) * 128)
+            for side, ref in enumerate((gate_ref, up_ref)):
+                value = restore(ref[rows, :])
+                for copy in range(2):
+                    out_ref[2 * half + copy, 0, tile * 128 : (tile + 1) * 128, side * 128 : (side + 1) * 128] = value
+
+
+def pack(gate_master, up_master):
     return pl.pallas_call(
         pack_kernel,
         grid=(4,),
-        in_specs=[
-            pl.BlockSpec(memory_space=pltpu.SMEM),
-            pl.BlockSpec((2 * FEATS, 128), lambda i: (i, 0)),
-            pl.BlockSpec((2 * FEATS, 128), lambda i: (i, 0)),
-        ],
-        out_specs=[pl.BlockSpec((1, FEATS, 256), lambda i: (i, 0, 0))] * 2,
-        out_shape=[shape, shape],
+        in_specs=[pl.BlockSpec((2 * FEATS, 128), lambda i: (i, 0))] * 2,
+        out_specs=pl.BlockSpec((4, 1, FEATS, 256), lambda i: (0, i, 0, 0)),
+        out_shape=jax.ShapeDtypeStruct((4, 4, FEATS, 256), BF),
         compiler_params=pltpu.CompilerParams(vmem_limit_bytes=VMEM_BYTES),
         name="pack",
-    )(yl, gate_master, up_master)
-
-
-def partial_kernel(y_ref, own_ref, other_ref, w00_ref, w01_ref, w10_ref, w11_ref, out_ref):
-    yl, yh = y_ref[0], y_ref[1]
+    )(gate_master, up_master)
+
+
+def offset(apart, zl):
+    reach = (6, 4, 0, 2)[apart]
+    return zl - reach if zl < 2 else zl + reach
+
+
+def partial_kernel(x_ref, own_ref, other_ref, w_ref, out_ref):
+    x = x_ref[0]
     index = lax.broadcasted_iota(jnp.int32, (EXTRA, ROWS), 0)
-    left = [jnp.zeros((EXTRA, ROWS), F32) for _ in range(4)]
-    right = [jnp.zeros((EXTRA, ROWS), F32) for _ in range(4)]
-    for part, a_ref in enumerate((own_ref, other_ref)):
-        for pool in range(4):
+    places = [[lax.rem(4 * x + 16 + offset(apart, zl), 16) for zl in range(4)] for apart in range(4)]
+    pools = [lax.rem(x + apart, 4) for apart in range(4)]
+    for apart in range(4):
+        left = jnp.zeros((EXTRA, ROWS), F32)
+        right = jnp.zeros((EXTRA, ROWS), F32)
+        for part, a_ref in enumerate((own_ref, other_ref)):
             square = jnp.zeros((1, ROWS), F32)
-            for block in range(4):
-                tail = a_ref[pool, block, LIVE:, :].astype(F32)
+            for zl in range(4):
+                tail = a_ref[places[apart][zl], LIVE:, :].astype(F32)
                 square = square + tail[0:1, ROWS:] + tail[1:2, :ROWS] + tail[1:2, ROWS:]
-            live = a_ref[pool, 0, LIVE:, :].astype(F32)[0:1, :ROWS]
+            live = tail[0:1, :ROWS]
             hi, mid, lo = split3(square)
             top, low = index == 2 * part, index == 2 * part + 1
-            left[pool] = jnp.where(top, live, jnp.where(low, mid, left[pool]))
-            right[pool] = jnp.where(top, hi, jnp.where(low, lo, right[pool]))
-    for flip_l, flip_h, w_ref in ((0, 0, w00_ref), (0, 1, w01_ref), (1, 0, w10_ref), (1, 1, w11_ref)):
-        to_l, to_h = lax.rem(yl + flip_l, 2), lax.rem(yh + flip_h, 2)
-        for part, a_ref in enumerate((own_ref, other_ref)):
-            total = jnp.zeros((4 * LIVE, 256), F32)
-            for block in range(4):
-                rows = a_ref[:, block, 0:LIVE, :].reshape(4 * LIVE, FEATS)
-                total = total + jnp.dot(rows, w_ref[block], preferred_element_type=F32)
-            for pool in range(4):
-                out_ref[to_l, pool, to_h, part * LIVE : (part + 1) * LIVE, :] = total[
-                    pool * LIVE : (pool + 1) * LIVE, :
-                ].astype(BF)
-        for pool in range(4):
-            out_ref[to_l, pool, to_h, 2 * LIVE :, 0:ROWS] = left[pool].astype(BF)
-            out_ref[to_l, pool, to_h, 2 * LIVE :, ROWS:] = right[pool].astype(BF)
-
-
-def partial(place, own, other, weights):
+            left = jnp.where(top, live, jnp.where(low, mid, left))
+            right = jnp.where(top, hi, jnp.where(low, lo, right))
+        for to_l in range(2):
+            for to_h in range(2):
+                out_ref[to_l, pools[apart], to_h, 2 * LIVE :, 0:ROWS] = left.astype(BF)
+                out_ref[to_l, pools[apart], to_h, 2 * LIVE :, ROWS:] = right.astype(BF)
+    for part, a_ref in enumerate((own_ref, other_ref)):
+        rows = [
+            jnp.concatenate([a_ref[places[apart][zl], 0:LIVE, :] for apart in range(4)], axis=0) for zl in range(4)
+        ]
+        for to_l in range(2):
+            for to_h in range(2):
+                total = jnp.zeros((4 * LIVE, 256), F32)
+                for zl in range(4):
+                    total = total + jnp.dot(rows[zl], w_ref[2 * to_l + to_h, zl], preferred_element_type=F32)
+                for apart in range(4):
+                    out_ref[to_l, pools[apart], to_h, part * LIVE : (part + 1) * LIVE, :] = total[
+                        apart * LIVE : (apart + 1) * LIVE, :
+                    ].astype(BF)
+
+
+def partial(x, own, other, weights):
     return pl.pallas_call(
         partial_kernel,
-        in_specs=[pl.BlockSpec(memory_space=pltpu.SMEM)] + [pl.BlockSpec(memory_space=pltpu.VMEM)] * 6,
+        in_specs=[pl.BlockSpec(memory_space=pltpu.SMEM)] + [pl.BlockSpec(memory_space=pltpu.VMEM)] * 3,
         out_specs=pl.BlockSpec(memory_space=pltpu.VMEM),
         out_shape=jax.ShapeDtypeStruct((2, 4, 2, CHUNK_ROWS, 256), BF),
         compiler_params=pltpu.CompilerParams(vmem_limit_bytes=VMEM_BYTES),
         name="partial",
-    )(place, own, other, *weights)
+    )(x, own, other, weights)
 
 
 def finish_kernel(c_ref, in_ref, out_ref):
@@ -184,22 +190,27 @@
     )(c, received)
 
 
+def slab_moves():
+    moves = []
+    for p in range(4):
+        for apart in range(4):
+            for zl in range(4):
+                moves.append(((4 * p + zl) * 4 + (p + apart) % 4, (4 * p + offset(apart, zl)) % 16 * 4 + p))
+    return moves
+
+
 def shards(gate_master, up_master, stream, norm_gain, live_rows):
-    yl = lax.axis_index("yl")
-    place = jnp.stack([yl, lax.axis_index("yh")]).astype(jnp.int32)
     core = lax.axis_index("c").astype(jnp.int32).reshape(1)
+    x = lax.axis_index("x").astype(jnp.int32).reshape(1)
     block = compact(stream, norm_gain, live_rows)
-    swap = [(zh * 4 + x, x * 4 + zh) for zh in range(4) for x in range(4)]
-    block = lax.ppermute(block, ("zh", "x"), swap)
-    same, flip = pack(yl.astype(jnp.int32).reshape(1), gate_master, up_master)
-    block, same, flip = lax.optimization_barrier((block, same, flip))
-    w01 = lax.ppermute(same, "yh", [(0, 1), (1, 0)])
-    w10 = lax.ppermute(flip, "yl", [(0, 1), (1, 0)])
-    w11 = lax.ppermute(flip, ("yl", "yh"), [(0, 3), (1, 2), (2, 1), (3, 0)])
-    own = lax.all_gather(block, ("zh", "zl"), axis=0, tiled=False).reshape(4, 4, BLOCK_ROWS, FEATS)
-    own, w01, w10, w11 = lax.optimization_barrier((own, w01, w10, w11))
+    block = lax.ppermute(block, ("zh", "zl", "x"), slab_moves())
+    weights = pack(gate_master, up_master)
+    block, weights = lax.optimization_barrier((block, weights))
+    weights = lax.all_to_all(weights, ("yl", "yh"), 0, 0)
+    own = lax.all_gather(block, ("zh", "zl"), axis=0, tiled=False)
+    own, weights = lax.optimization_barrier((own, weights))
     other = lax.ppermute(own, "c", [(0, 1), (1, 0)])
-    sums = partial(place, own, other, (same, w01, w10, w11))
+    sums = partial(x, own, other, weights)
     sums = sums.reshape(16, CHUNK_ROWS, 256)
     received = lax.all_to_all(sums, ("yl", "x", "yh"), 0, 0)
     return finish(core, received.reshape(2, 4, 2, CHUNK_ROWS, 256))

time: 103 us -> 91.7 us (0.89)
  blocking collectives: 42.1 us -> 25.3 us
  starting transfers between devices: 28.1 us -> 32.5 us
  local copies, waits for them, and re-layouts: 2.45 us -> 3.78 us
    all_gather x1, blocking collectives: 42.1 us -> 25.3 us  [shards(): own = lax.all_gather(block, ('zh', 'zl'), axis=0, tiled=False)]
    all_to_all x0 -> x1, starting transfers between devices: none -> 4.18 us  [shards(): weights = lax.all_to_all(weights, ('yl', 'yh'), 0, 0)]
    ppermute x4 -> x1, starting transfers between devices: 11.7 us -> 15.4 us  [shards(): block = lax.ppermute(block, ('zh', 'zl', 'x'), slab_moves())]
    ppermute x1, starting transfers between devices: 9.64 us -> 7.35 us  [shards(): other = lax.ppermute(own, 'c', [(0, 1), (1, 0)])]
    unnamed x4 -> x6, local copies, waits for them, and re-layouts: 2.45 us -> 3.78 us
    all_to_all x1, starting transfers between devices: 6.78 us -> 5.56 us  [shards(): received = lax.all_to_all(sums, ('yl', 'x', 'yh'), 0, 0)]
  transfers between devices with their start and end apart: 6 -> 4, of which waited for: 2 -> 3; matrix products, arithmetic and copies ran while one was open for 0% -> 0% of each run, Pallas kernels for 3% -> 3%
where the time goes in v2:
time: 91.7 us; the launch traced here: 90.9 us
  starting transfers between devices  32.5 us (35%)
  blocking collectives  25.3 us (28%)
  waiting for transfers between devices  20.5 us (22%)
  Pallas kernels  8.7 us (9%)
  local copies, waits for them, and re-layouts  3.78 us (4%)
    all_gather x1, blocking collectives, shards(): own = lax.all_gather(block, ('zh', 'zl'), axis=0, tiled=False)  25.3 us
    all_to_all x1, waiting for transfers between devices, shards(): received = lax.all_to_all(sums, ('yl', 'x', 'yh'), 0, 0)  18.1 us
    ppermute x1, starting transfers between devices, shards(): block = lax.ppermute(block, ('zh', 'zl', 'x'), slab_moves())  15.4 us
    ppermute x1, starting transfers between devices, shards(): other = lax.ppermute(own, 'c', [(0, 1), (1, 0)])  7.35 us
    all_to_all x1, starting transfers between devices, shards(): received = lax.all_to_all(sums, ('yl', 'x', 'yh'), 0, 0)  5.56 us
    all_to_all x1, starting transfers between devices, shards(): weights = lax.all_to_all(weights, ('yl', 'yh'), 0, 0)  4.18 us
    unnamed x6, local copies, waits for them, and re-layouts  3.78 us
    pallas_call x1, Pallas kernels, pack(): pl.pallas_call(pack_kernel, grid=(4,), in_specs=[pl.BlockSpec((2 * FEATS,...  2.88 us
  transfers between devices with their start and end apart: 4, of which 3 were waited for; matrix products, arithmetic and copies ran while one was open for 0% of the time, Pallas kernels for 3%

profile of v2, /device:TPU:1, one launch (start us, length us, event | category | flops | bytes accessed | tf_op | source)
XLA Modules:
  0.0 90.9 jit_solution(15283773207341114152)
XLA Ops:
  0.0 1.8 %compact.1 = bf16[72,256]{1,0:T(8,128)(2,1)} custom-call(f32[128,256]{1,0:T(8,128)} %stream_ref.1, f32[1,256]{1,0:T(1,128)} %bitcast.10, s32[1,128]{1,0:T(1,128)} %bitcast.11), custom_call_target="tpu_custom_call" | custom-call | tf_op jit(solution)/shard_map/compact/pallas_call | solution.py:58
  1.8 15.4 %collective-permute-start = (bf16[72,256]{1,0:T(8,128)(2,1)}, bf16[72,256]{1,0:T(8,128)(2,1)S(1)}, u32[]{:S(2)}, u32[]{:S(2)}) collective-permute-start(bf16[72,256]{1,0:T(8,128)(2,1)} %compact.1), channel_id=1, source_target_pairs={{0,320},{32,352},{64,256},{96,288},{4,384},{36,416},{68,192},{100,... | collective-permute-start | bytes 110600 | tf_op jit(solution)/shard_map/ppermute | solution.py:206
  17.2 0.0 copy-start.1
  17.2 1.2 %copy-done.1 = f32[2048,128]{1,0:T(8,128)S(1)} copy-done((f32[2048,128]{1,0:T(8,128)S(1)}, f32[2048,128]{1,0:T(8,128)}, u32[]{:S(2)}) %copy-start.1) | copy-done | bytes 1048600
  18.4 0.0 copy-start.2
  18.4 1.2 %copy-done.2 = f32[2048,128]{1,0:T(8,128)S(1)} copy-done((f32[2048,128]{1,0:T(8,128)S(1)}, f32[2048,128]{1,0:T(8,128)}, u32[]{:S(2)}) %copy-start.2) | copy-done | bytes 1048600
  19.6 2.9 %pack.1 = bf16[4,4,256,256]{3,2,1,0:T(8,128)(2,1)S(1)} custom-call(f32[2048,128]{1,0:T(8,128)S(1)} %copy-done.1, f32[2048,128]{1,0:T(8,128)S(1)} %copy-done.2), custom_call_target="tpu_custom_call" | custom-call | tf_op jit(solution)/shard_map/pack/pallas_call | solution.py:91
  22.5 0.0 copy-start
  22.5 1.3 %copy-done = bf16[4,4,256,256]{3,2,1,0:T(8,128)(2,1)} copy-done((bf16[4,4,256,256]{3,2,1,0:T(8,128)(2,1)}, bf16[4,4,256,256]{3,2,1,0:T(8,128)(2,1)S(1)}, u32[]{:S(2)}) %copy-start) | copy-done | bytes 2097176
  23.9 0.0 collective-permute-done
  23.9 4.2 %all-to-all-start = ((bf16[4,4,256,256]{3,2,1,0:T(8,128)(2,1)}), bf16[4,4,256,256]{3,2,1,0:T(8,128)(2,1)S(1)}, u32[]{:S(2)}, u32[]{:S(2)}) async-start(bf16[4,4,256,256]{3,2,1,0:T(8,128)(2,1)} %copy-done), calls=%async_computation | async-start | bytes 4194304 | tf_op jit(solution)/shard_map/all_to_all | solution.py:209
  28.1 25.3 %all-gather = bf16[1152,256]{1,0:T(8,128)(2,1)S(1)} all-gather(bf16[72,256]{1,0:T(8,128)(2,1)S(1)} %collective-permute-done), channel_id=2, replica_groups=mesh['zh'=4,'zl'=4,'yl'=2,'x'=4,'yh'=2,'c'=2] {'zh','zl'}, dimensions={0}, use_global_device_ids=true | all-gather | bytes 626688 | tf_op jit(solution)/shard_map/all_gather | solution.py:210
  53.4 0.8 all-to-all-done.w_ref
  54.2 7.3 %collective-permute-start.1 = (bf16[16,72,256]{2,1,0:T(8,128)(2,1)S(1)}, bf16[16,72,256]{2,1,0:T(8,128)(2,1)S(1)}, u32[]{:S(2)}, u32[]{:S(2)}) collective-permute-start(bf16[16,72,256]{2,1,0:T(8,128)(2,1)S(1)} %bitcast.8), channel_id=1, source_target_pairs={{0,1},{1,0},{2,3},{3,2},{4,5},{5,4},{6,7},{7,6},{8,9},{9,8},{10,11... | collective-permute-start | bytes 1769480 | tf_op jit(solution)/shard_map/ppermute | solution.py:212
  61.5 1.6 %collective-permute-done.1.other_ref = bf16[16,72,256]{2,1,0:T(8,128)(2,1)S(1)} collective-permute-done((bf16[16,72,256]{2,1,0:T(8,128)(2,1)S(1)}, bf16[16,72,256]{2,1,0:T(8,128)(2,1)S(1)}, u32[]{:S(2)}, u32[]{:S(2)}) %collective-permute-start.1) | collective-permute-done | bytes 589856 | tf_op jit(solution)/shard_map/ppermute | solution.py:212
  63.2 2.3 %partial.1 = bf16[2,4,2,136,256]{4,3,2,1,0:T(8,128)(2,1)} custom-call(s32[1]{0:T(128)} %bitcast.1.x_ref, bf16[16,72,256]{2,1,0:T(8,128)(2,1)S(1)} %bitcast.9, bf16[16,72,256]{2,1,0:T(8,128)(2,1)S(1)} %collective-permute-done.1.other_ref, bf16[4,4,256,256]{3,2,1,0:T(8,128)(2,1)S(1)} %all-to-all-done.w_ref), custom_call_target="tpu_custom_call" | custom-call | tf_op jit(solution)/shard_map/partial/pallas_call | solution.py:145
  65.4 5.6 %all-to-all-start.1 = ((bf16[16,136,256]{2,1,0:T(8,128)(2,1)}), bf16[16,136,256]{2,1,0:T(8,128)(2,1)S(1)}, u32[]{:S(2)}, u32[]{:S(2)}) async-start(bf16[16,136,256]{2,1,0:T(8,128)(2,1)} %bitcast.5), calls=%async_computation.1 | async-start | bytes 2228224 | tf_op jit(solution)/shard_map/all_to_all | solution.py:215
  71.0 18.1 %all-to-all-done.1 = bf16[16,136,256]{2,1,0:T(8,128)(2,1)S(1)} async-done(((bf16[16,136,256]{2,1,0:T(8,128)(2,1)}), bf16[16,136,256]{2,1,0:T(8,128)(2,1)S(1)}, u32[]{:S(2)}, u32[]{:S(2)}) %all-to-all-start.1) | async-done | bytes 1114144 | tf_op jit(solution)/shard_map/all_to_all | solution.py:215
  89.1 1.8 %finish.1 = bf16[512,128]{1,0:T(8,128)(2,1)} custom-call(s32[1]{0:T(128)} %bitcast.c_ref, bf16[2,4,2,136,256]{4,3,2,1,0:T(8,128)(2,1)S(1)} %bitcast.7), custom_call_target="tpu_custom_call" | custom-call | tf_op jit(solution)/shard_map/finish/pallas_call | solution.py:183
Async XLA Ops:
  1.8 22.1 %collective-permute-start = (bf16[72,256]{1,0:T(8,128)(2,1)}, bf16[72,256]{1,0:T(8,128)(2,1)S(1)}, u32[]{:S(2)}, u32[]{:S(2)}) collective-permute-start(bf16[72,256]{1,0:T(8,128)(2,1)} %compact.1), channel_id=1, source_target_pairs={{0,320},{32,352},{64,256},{96,288},{4,384},{36,416},{68,192},{100,... | collective-permute-start | bytes 110600 | tf_op jit(solution)/shard_map/ppermute | solution.py:206
  17.2 1.2 %copy-start.1 = (f32[2048,128]{1,0:T(8,128)S(1)}, f32[2048,128]{1,0:T(8,128)}, u32[]{:S(2)}) copy-start(f32[2048,128]{1,0:T(8,128)} %gate_ref.1) | copy-start | bytes 3145732
  18.4 1.2 %copy-start.2 = (f32[2048,128]{1,0:T(8,128)S(1)}, f32[2048,128]{1,0:T(8,128)}, u32[]{:S(2)}) copy-start(f32[2048,128]{1,0:T(8,128)} %up_ref.1) | copy-start | bytes 3145732
  22.5 1.3 %copy-start = (bf16[4,4,256,256]{3,2,1,0:T(8,128)(2,1)}, bf16[4,4,256,256]{3,2,1,0:T(8,128)(2,1)S(1)}, u32[]{:S(2)}) copy-start(bf16[4,4,256,256]{3,2,1,0:T(8,128)(2,1)S(1)} %pack.1) | copy-start | bytes 6291460
  23.9 30.3 %all-to-all-start = ((bf16[4,4,256,256]{3,2,1,0:T(8,128)(2,1)}), bf16[4,4,256,256]{3,2,1,0:T(8,128)(2,1)S(1)}, u32[]{:S(2)}, u32[]{:S(2)}) async-start(bf16[4,4,256,256]{3,2,1,0:T(8,128)(2,1)} %copy-done), calls=%async_computation | async-start | bytes 4194304 | tf_op jit(solution)/shard_map/all_to_all | solution.py:209
  54.2 9.0 %collective-permute-start.1 = (bf16[16,72,256]{2,1,0:T(8,128)(2,1)S(1)}, bf16[16,72,256]{2,1,0:T(8,128)(2,1)S(1)}, u32[]{:S(2)}, u32[]{:S(2)}) collective-permute-start(bf16[16,72,256]{2,1,0:T(8,128)(2,1)S(1)} %bitcast.8), channel_id=1, source_target_pairs={{0,1},{1,0},{2,3},{3,2},{4,5},{5,4},{6,7},{7,6},{8,9},{9,8},{10,11... | collective-permute-start | bytes 1769480 | tf_op jit(solution)/shard_map/ppermute | solution.py:212
  65.4 23.7 %all-to-all-start.1 = ((bf16[16,136,256]{2,1,0:T(8,128)(2,1)}), bf16[16,136,256]{2,1,0:T(8,128)(2,1)S(1)}, u32[]{:S(2)}, u32[]{:S(2)}) async-start(bf16[16,136,256]{2,1,0:T(8,128)(2,1)} %bitcast.5), calls=%async_computation.1 | async-start | bytes 2228224 | tf_op jit(solution)/shard_map/all_to_all | solution.py:215

commit v3 on v0

v3 whole, which is shorter than its diff:
```python
import jax
import jax.numpy as jnp
from jax import lax
from jax.experimental import pallas as pl
from jax.experimental.pallas import tpu as pltpu
from jax.sharding import Mesh, PartitionSpec as P

D = 8192
LIVE = 64
ROWS = 128
FEATS = 256
EXTRA = 8
BLOCK_ROWS = LIVE + EXTRA
AXES = ("zh", "zl", "yl", "x", "yh", "c")
BF = jnp.bfloat16
F32 = jnp.float32
VMEM_BYTES = 24 * 1024 * 1024


def split3(value):
    hi = value.astype(BF).astype(F32)
    mid = (value - hi).astype(BF).astype(F32)
    lo = (value - hi - mid).astype(BF).astype(F32)
    return hi, mid, lo


def diagonal(size):
    return lax.broadcasted_iota(jnp.int32, (size, size), 0) == lax.broadcasted_iota(jnp.int32, (size, size), 1)


def slot_table(live):
    rows = lax.broadcasted_iota(jnp.int32, (ROWS, ROWS), 0)
    cols = lax.broadcasted_iota(jnp.int32, (ROWS, ROWS), 1)
    before = jnp.where(rows <= cols, 1.0, 0.0).astype(BF)
    wide = jnp.broadcast_to(live, (16, ROWS))
    rank = jnp.dot(wide.astype(BF), before, preferred_element_type=F32)[0:1, :]
    slot = lax.broadcasted_iota(jnp.int32, (LIVE, ROWS), 0).astype(F32) + 1.0
    return jnp.where((slot == rank) & (live > 0.5), 1.0, 0.0)


def restore(master):
    tile = master.T.reshape(4, 32, 128)
    size = jnp.abs(tile)
    largest = jnp.max(size, axis=1, keepdims=True)
    wide = largest * 8388609.0
    power = jnp.abs(wide - wide * (1.0 - 2.0**-24))
    power = jnp.where(power > largest, power * 0.5, power)
    power = jnp.where(power * 2.0 <= largest, power * 2.0, power)
    scale = jnp.clip(power, 2.0**-32, 2.0**4) * 0.25
    level = jnp.zeros_like(size)
    for edge, value in ((0.25, 0.5), (0.75, 1.0), (1.25, 1.5), (1.75, 2.0), (2.5, 3.0), (3.5, 4.0), (5.0, 6.0)):
        level = jnp.where(size >= scale * edge, scale * value, level)
    return jnp.where(tile < 0.0, -level, level).reshape(128, 128).T.astype(BF)


def compact(stream, gain, live, block_ref):
    table = slot_table(live)
    scaled = (stream * gain).astype(BF)
    rows = jnp.dot(table.astype(BF), scaled, preferred_element_type=F32)
    block_ref[0:LIVE, :] = rows.astype(BF)
    square = jnp.sum(stream * stream, axis=1, keepdims=True)
    square_row = jnp.sum(jnp.where(diagonal(ROWS), square, 0.0), axis=0, keepdims=True)
    hi, mid, lo = split3(square_row)
    index = lax.broadcasted_iota(jnp.int32, (EXTRA, ROWS), 0)
    block_ref[LIVE:, 0:ROWS] = jnp.where(index == 0, live, jnp.where(index == 1, mid, 0.0)).astype(BF)
    block_ref[LIVE:, ROWS:] = jnp.where(index == 0, hi, jnp.where(index == 1, lo, 0.0)).astype(BF)


def prepare_kernel(
    gate_hbm, up_hbm, stream_hbm, gain_hbm, live_hbm, out_hbm, block_ref,
    gate_ref, up_ref, stream_ref, gain_ref, live_ref, packed_ref, row_sems, in_sems, out_sems,
):
    loads = []
    for zl in range(4):
        rows = pl.ds(zl * 2 * FEATS, 2 * FEATS)
        for side, (hbm, ref) in enumerate(((gate_hbm, gate_ref), (up_hbm, up_ref))):
            load = pltpu.make_async_copy(hbm.at[rows, :], ref.at[rows, :], in_sems.at[zl, side])
            load.start()
            loads.append(load)
    row_loads = []
    for i, (hbm, ref) in enumerate(((stream_hbm, stream_ref), (gain_hbm, gain_ref), (live_hbm, live_ref))):
        load = pltpu.make_async_copy(hbm, ref, row_sems.at[i])
        load.start()
        row_loads.append(load)
    stores = []
    for zl in range(4):
        for side, ref in enumerate((gate_ref, up_ref)):
            loads[2 * zl + side].wait()
            for tile in range(4):
                yl, top = tile // 2, (tile % 2) * 128
                value = restore(ref[zl * 2 * FEATS + tile * 128 : zl * 2 * FEATS + (tile + 1) * 128, :])
                packed_ref[yl, zl, top : top + 128, side * 128 : (side + 1) * 128] = value
        for yl in range(2):
            for x in range(4):
                store = pltpu.make_async_copy(packed_ref.at[yl, zl], out_hbm.at[4 * yl + x, zl], out_sems.at[zl, yl, x])
                store.start()
                stores.append(store)
    for load in row_loads:
        load.wait()
    compact(stream_ref[...], gain_ref[...], live_ref[...].astype(F32), block_ref)
    for store in stores:
        store.wait()


def prepare(gate_master, up_master, stream, gain, live):
    return pl.pallas_call(
        prepare_kernel,
        in_specs=[pl.BlockSpec(memory_space=pl.ANY)] * 5,
        out_specs=[pl.BlockSpec(memory_space=pl.ANY), pl.BlockSpec(memory_space=pltpu.VMEM)],
        out_shape=[jax.ShapeDtypeStruct((8, 4, FEATS, 256), BF), jax.ShapeDtypeStruct((BLOCK_ROWS, FEATS), BF)],
        scratch_shapes=[
            pltpu.VMEM((8 * FEATS, 128), F32),
            pltpu.VMEM((8 * FEATS, 128), F32),
            pltpu.VMEM((ROWS, FEATS), F32),
            pltpu.VMEM((1, FEATS), F32),
            pltpu.VMEM((1, ROWS), jnp.int32),
            pltpu.VMEM((2, 4, FEATS, 256), BF),
            pltpu.SemaphoreType.DMA((3,)),
            pltpu.SemaphoreType.DMA((4, 2)),
            pltpu.SemaphoreType.DMA((4, 2, 4)),
        ],
        compiler_params=pltpu.CompilerParams(vmem_limit_bytes=62 * 1024 * 1024),
        name="prepare",
    )(gate_master, up_master, stream, gain.reshape(1, FEATS), live.reshape(1, ROWS))


def add_up(a_refs, own_ref, sent_ref, square_ref, table_ref, weight):
    index = lax.broadcasted_iota(jnp.int32, (EXTRA, ROWS), 0)
    for i, a_ref in enumerate(a_refs):
        tails = jnp.sum(a_ref[:, LIVE:, :].astype(F32), axis=0)
        square = tails[0:1, ROWS:] + tails[1:2, :ROWS] + tails[1:2, ROWS:]
        hi, mid, lo = split3(square)
        sent_ref[i, LIVE:, 0:ROWS] = jnp.where(index == 1, mid, 0.0).astype(BF)
        sent_ref[i, LIVE:, ROWS:] = jnp.where(index == 0, hi, jnp.where(index == 1, lo, 0.0)).astype(BF)
        square_ref[i] = jnp.broadcast_to(square, (EXTRA, ROWS))
        table_ref[i] = slot_table(a_ref[0, LIVE:, :].astype(F32)[0:1, :ROWS]).astype(BF)
    totals = [jnp.zeros((2 * LIVE, 256), F32) for _ in range(2)]
    for z in range(16):
        rows = jnp.concatenate([a_ref[z, 0:LIVE, :] for a_ref in a_refs], axis=0)
        for other in range(2):
            totals[other] = totals[other] + jnp.dot(rows, weight(other, z), preferred_element_type=F32)
    for i in range(2):
        own_ref[i] = totals[0][i * LIVE : (i + 1) * LIVE, :]
        sent_ref[i, 0:LIVE, :] = totals[1][i * LIVE : (i + 1) * LIVE, :].astype(BF)


def near_kernel(yl_ref, own_a_ref, other_a_ref, w_hbm, own_ref, sent_ref, square_ref, table_ref, w_ref, sems):
    yl = yl_ref[0]
    loads = []
    for x in range(4):
        for other in range(2):
            load = pltpu.make_async_copy(w_hbm.at[4 * (yl ^ other) + x], w_ref.at[4 * other + x], sems.at[x, other])
            load.start()
            loads.append(load)

    def weight(other, z):
        if z % 4 == 0:
            loads[2 * (z // 4) + other].wait()
        return w_ref[4 * other + z // 4, z % 4]

    add_up((own_a_ref, other_a_ref), own_ref, sent_ref, square_ref, table_ref, weight)


def far_kernel(place_ref, own_a_ref, other_a_ref, near_ref, w_ref, own_ref, sent_ref, square_ref, table_ref, far_ref):
    yh, c = place_ref[0], place_ref[1]
    add_up(
        (own_a_ref, other_a_ref), own_ref, far_ref, square_ref, table_ref, lambda other, z: w_ref[4 * other + z // 4, z % 4]
    )
    for flip_h, ref in enumerate((near_ref, far_ref)):
        for flip_c in range(2):
            sent_ref[yh ^ flip_h, c ^ flip_c] = ref[flip_c]


SUM_SHAPES = [
    jax.ShapeDtypeStruct((2, LIVE, 256), F32),
    jax.ShapeDtypeStruct((2, BLOCK_ROWS, 256), BF),
    jax.ShapeDtypeStruct((2, EXTRA, ROWS), F32),
    jax.ShapeDtypeStruct((2, LIVE, ROWS), BF),
]


def near(yl, own_a, other_a, weights):
    vmem = pl.BlockSpec(memory_space=pltpu.VMEM)
    return pl.pallas_call(
        near_kernel,
        in_specs=[pl.BlockSpec(memory_space=pltpu.SMEM), vmem, vmem, pl.BlockSpec(memory_space=pl.ANY)],
        out_specs=[vmem] * 5,
        out_shape=SUM_SHAPES + [jax.ShapeDtypeStruct(weights.shape, BF)],
        scratch_shapes=[pltpu.SemaphoreType.DMA((4, 2))],
        compiler_params=pltpu.CompilerParams(vmem_limit_bytes=VMEM_BYTES),
        name="near",
    )(yl, own_a, other_a, weights)


def far(place, own_a, other_a, near_sent, weights):
    vmem = pl.BlockSpec(memory_space=pltpu.VMEM)
    return pl.pallas_call(
        far_kernel,
        in_specs=[pl.BlockSpec(memory_space=pltpu.SMEM)] + [vmem] * 4,
        out_specs=[vmem] * 4,
        out_shape=[SUM_SHAPES[0], jax.ShapeDtypeStruct((2, 2, BLOCK_ROWS, 256), BF), SUM_SHAPES[2], SUM_SHAPES[3]],
        scratch_shapes=[pltpu.VMEM((2, BLOCK_ROWS, 256), BF)],
        compiler_params=pltpu.CompilerParams(vmem_limit_bytes=VMEM_BYTES),
        name="far",
    )(place, own_a, other_a, near_sent, weights)


def finish_kernel(place_ref, *refs):
    yh, c = place_ref[0], place_ref[1]
    other_ref, out_ref = refs[6], refs[7]
    for flip_h in range(2):
        own_ref, square_ref, table_ref = refs[3 * flip_h : 3 * flip_h + 3]
        for flip_c in range(2):
            sent = other_ref[yh ^ flip_h, c ^ flip_c].astype(F32)
            rows = own_ref[flip_c] + sent[0:LIVE, :]
            tail = sent[LIVE:, :]
            square = square_ref[flip_c, 0:1, :] + tail[0:1, ROWS:] + tail[1:2, :ROWS] + tail[1:2, ROWS:]
            table = table_ref[flip_c]
            inverse = lax.rsqrt(square * (1.0 / D) + 1e-06)
            rows = rows * jnp.sum(table.astype(F32) * inverse, axis=1, keepdims=True)
            gate, up = rows[:, :128], rows[:, 128:]
            hidden = (gate / (1.0 + jnp.exp(-gate)) * up).astype(BF)
            spread = lax.dot_general(table, hidden, (((0,), (0,)), ((), ())), preferred_element_type=F32)
            block = 2 * (yh ^ flip_h) + (c ^ flip_c)
            out_ref[pl.ds(pl.multiple_of(block * ROWS, ROWS), ROWS), :] = spread.astype(BF)


def finish(place, near_sums, far_sums, other):
    return pl.pallas_call(
        finish_kernel,
        in_specs=[pl.BlockSpec(memory_space=pltpu.SMEM)] + [pl.BlockSpec(memory_space=pltpu.VMEM)] * 7,
        out_specs=pl.BlockSpec(memory_space=pltpu.VMEM),
        out_shape=jax.ShapeDtypeStruct((4 * ROWS, 128), BF),
        compiler_params=pltpu.CompilerParams(vmem_limit_bytes=VMEM_BYTES),
        name="finish",
    )(place, *near_sums, *far_sums, other)


def partner_groups():
    return [
        [((yl * 4 + x) * 2 + (h ^ (yl & c))) * 2 + c for yl in range(2) for x in range(4)]
        for h in range(2)
        for c in range(2)
    ]


def partner_moves():
    moves = []
    for yl in range(2):
        for yh in range(2):
            for c in range(2):
                moves.append(((yl * 2 + yh) * 2 + c, ((1 - yl) * 2 + (yh ^ c)) * 2 + c))
    return moves


def shards(gate_master, up_master, stream, norm_gain, live_rows):
    yl = lax.axis_index("yl").astype(jnp.int32).reshape(1)
    place = jnp.stack([lax.axis_index("yh"), lax.axis_index("c")]).astype(jnp.int32)
    weights, block = prepare(gate_master, up_master, stream, norm_gain, live_rows)
    weights = lax.all_to_all(weights, ("yl", "x", "yh", "c"), 0, 0, axis_index_groups=partner_groups())
    a00 = lax.all_gather(block, ("zh", "zl"), axis=0, tiled=False)
    a10 = lax.ppermute(a00, "yh", [(0, 1), (1, 0)])
    a01 = lax.ppermute(a00, "c", [(0, 1), (1, 0)])
    a11 = lax.ppermute(a10, "c", [(0, 1), (1, 0)])
    near_own, near_sent, near_square, near_table, weights = near(yl, a00, a01, weights)
    far_own, sent, far_square, far_table = far(place, a10, a11, near_sent, weights)
    other = lax.ppermute(sent, ("yl", "yh", "c"), partner_moves())
    return finish(place, (near_own, near_square, near_table), (far_own, far_square, far_table), other)


def solution(mesh):
    fine = Mesh(mesh.devices.reshape(4, 4, 2, 4, 2, 2), AXES)
    learner, tp = ("zh", "zl", "yl"), ("yh", "c")
    placed = (
        P("x", learner + tp),
        P("x", learner + tp),
        P(("x",) + tp, learner),
        P(learner),
        P(("x",) + tp),
    )
    return jax.shard_map(shards, mesh=fine, in_specs=placed, out_specs=P("x", learner + tp), check_vma=False)
```

time: 360 us -> 87.8 us (0.24)
  the two profiles are of different devices: /device:TPU:28 before, /device:TPU:1 now
where the time goes in v3:
time: 87.8 us; the launch traced here: 87.4 us
  blocking collectives  34.9 us (40%)
  starting transfers between devices  25.4 us (29%)
  waiting for transfers between devices  15.1 us (17%)
  Pallas kernels  11.8 us (13%)
    all_gather x1, blocking collectives, shards(): a00 = lax.all_gather(block, ('zh', 'zl'), axis=0, tiled=False)  34.9 us
    ppermute x1, waiting for transfers between devices, shards(): a10 = lax.ppermute(a00, 'yh', [(0, 1), (1, 0)])  11.4 us
    ppermute x1, starting transfers between devices, shards(): a01 = lax.ppermute(a00, 'c', [(0, 1), (1, 0)])  7.77 us
    all_to_all x1, starting transfers between devices, shards(): lax.all_to_all(weights, ('yl', 'x', 'yh', 'c'), 0, 0, axis_index_groups=p...  7.31 us
    pallas_call x1, Pallas kernels, prepare(): pl.pallas_call(prepare_kernel, in_specs=[pl.BlockSpec(memory_space=pl.ANY...  6.45 us
    ppermute x1, starting transfers between devices, shards(): a11 = lax.ppermute(a10, 'c', [(0, 1), (1, 0)])  4.54 us
    ppermute x1, waiting for transfers between devices, shards(): other = lax.ppermute(sent, ('yl', 'yh', 'c'), partner_moves())  3.73 us
    ppermute x1, starting transfers between devices, shards(): other = lax.ppermute(sent, ('yl', 'yh', 'c'), partner_moves())  3.36 us
  transfers between devices with their start and end apart: 5, of which 2 were waited for; matrix products, arithmetic and copies ran while one was open for 0% of the time, Pallas kernels for 3%

profile of v3, /device:TPU:1, one launch (start us, length us, event | category | flops | bytes accessed | tf_op | source)
XLA Modules:
  0.0 87.4 jit_solution(15667079316245492958)
XLA Ops:
  0.0 6.5 %prepare.1 = (bf16[8,4,256,256]{3,2,1,0:T(8,128)(2,1)}, bf16[72,256]{1,0:T(8,128)(2,1)}) custom-call(f32[2048,128]{1,0:T(8,128)} %gate_hbm.1, f32[2048,128]{1,0:T(8,128)} %up_hbm.1, f32[128,256]{1,0:T(8,128)} %stream_hbm.1, f32[1,256]{1,0:T(1,128)} %bitcast.9, s32[1,128]{1,0:T(1,128)} %bitcast.10), custom_call_target="tpu_custom_call" | custom-call | tf_op jit(solution)/shard_map/prepare/pallas_call | solution.py:106
  6.5 0.0 copy-start
  6.5 7.3 %all-to-all-start = ((bf16[8,4,256,256]{3,2,1,0:T(8,128)(2,1)}), bf16[8,4,256,256]{3,2,1,0:T(8,128)(2,1)}, u32[]{:S(2)}, u32[]{:S(2)}) async-start(bf16[8,4,256,256]{3,2,1,0:T(8,128)(2,1)} %get-tuple-element.17), calls=%async_computation | async-start | bytes 8388608 | tf_op jit(solution)/shard_map/all_to_all | solution.py:260
  13.8 0.0 copy-done
  13.8 34.9 %all-gather = bf16[1152,256]{1,0:T(8,128)(2,1)S(1)} all-gather(bf16[72,256]{1,0:T(8,128)(2,1)S(1)} %copy-done), channel_id=2, replica_groups=mesh['zh'=4,'zl'=4,'yl'=2,'x'=4,'yh'=2,'c'=2] {'zh','zl'}, dimensions={0}, use_global_device_ids=true | all-gather | bytes 626688 | tf_op jit(solution)/shard_map/all_gather | solution.py:261
  48.7 2.5 %collective-permute-start.1 = (bf16[16,72,256]{2,1,0:T(8,128)(2,1)S(1)}, bf16[16,72,256]{2,1,0:T(8,128)(2,1)S(1)}, u32[]{:S(2)}, u32[]{:S(2)}) collective-permute-start(bf16[16,72,256]{2,1,0:T(8,128)(2,1)S(1)} %bitcast.6), channel_id=1, source_target_pairs={{0,2},{2,0},{1,3},{3,1},{4,6},{6,4},{5,7},{7,5},{8,10},{10,8},{9,1... | collective-permute-start | bytes 1769480 | tf_op jit(solution)/shard_map/ppermute | solution.py:262
  51.1 7.8 %collective-permute-start = (bf16[16,72,256]{2,1,0:T(8,128)(2,1)S(1)}, bf16[16,72,256]{2,1,0:T(8,128)(2,1)S(1)}, u32[]{:S(2)}, u32[]{:S(2)}) collective-permute-start(bf16[16,72,256]{2,1,0:T(8,128)(2,1)S(1)} %bitcast.7), channel_id=1, source_target_pairs={{0,1},{1,0},{2,3},{3,2},{4,5},{5,4},{6,7},{7,6},{8,9},{9,8},{10,11... | collective-permute-start | bytes 1769480 | tf_op jit(solution)/shard_map/ppermute | solution.py:263
  58.9 11.4 %collective-permute-done.1.own_a_ref = bf16[16,72,256]{2,1,0:T(8,128)(2,1)S(1)} collective-permute-done((bf16[16,72,256]{2,1,0:T(8,128)(2,1)S(1)}, bf16[16,72,256]{2,1,0:T(8,128)(2,1)S(1)}, u32[]{:S(2)}, u32[]{:S(2)}) %collective-permute-start.1) | collective-permute-done | bytes 589856 | tf_op jit(solution)/shard_map/ppermute | solution.py:262
  70.3 4.5 %collective-permute-start.2 = (bf16[16,72,256]{2,1,0:T(8,128)(2,1)S(1)}, bf16[16,72,256]{2,1,0:T(8,128)(2,1)S(1)}, u32[]{:S(2)}, u32[]{:S(2)}) collective-permute-start(bf16[16,72,256]{2,1,0:T(8,128)(2,1)S(1)} %collective-permute-done.1.own_a_ref), channel_id=1, source_target_pairs={{0,1},{1,0},{2,3},{3,2},{4,5},{5,4},{6,7},{7,6},{8,9},{9,8},{10,11... | collective-permute-start | bytes 1769480 | tf_op jit(solution)/shard_map/ppermute | solution.py:264
  74.9 0.1 pad_add_fusion.place_ref
  75.0 0.0 collective-permute-done.other_a_ref
  75.0 0.0 all-to-all-done.w_hbm
  75.0 2.5 %near.1 = (f32[2,64,256]{2,1,0:T(8,128)S(1)}, bf16[2,72,256]{2,1,0:T(8,128)(2,1)S(1)}, f32[2,8,128]{2,1,0:T(8,128)S(1)}, bf16[2,64,128]{2,1,0:T(8,128)(2,1)S(1)}, bf16[8,4,256,256]{3,2,1,0:T(8,128)(2,1)S(1)}) custom-call(s32[1]{0:T(128)} %bitcast.2.yl_ref, bf16[16,72,256]{2,1,0:T(8,128)(2,1)S(1)} %bitcast.8, ...), custom_call_target="tpu_custom_call" | custom-call | tf_op jit(solution)/shard_map/near/pallas_call | solution.py:184
  77.5 0.0 collective-permute-done.2.other_a_ref
  77.5 1.3 %far.1 = (f32[2,64,256]{2,1,0:T(8,128)S(1)}, bf16[2,2,72,256]{3,2,1,0:T(8,128)(2,1)S(1)}, f32[2,8,128]{2,1,0:T(8,128)S(1)}, bf16[2,64,128]{2,1,0:T(8,128)(2,1)S(1)}) custom-call(s32[2]{0:T(128)S(1)} %pad_add_fusion.place_ref, bf16[16,72,256]{2,1,0:T(8,128)(2,1)S(1)} %collective-permute-done.1.own_a_ref, ...), custom_call_target="tpu_custom_call" | custom-call | tf_op jit(solution)/shard_map/far/pallas_call | solution.py:197
  78.8 3.4 %collective-permute-start.3 = (bf16[2,2,72,256]{3,2,1,0:T(8,128)(2,1)S(1)}, bf16[2,2,72,256]{3,2,1,0:T(8,128)(2,1)S(1)}, u32[]{:S(2)}, u32[]{:S(2)}) collective-permute-start(bf16[2,2,72,256]{3,2,1,0:T(8,128)(2,1)S(1)} %get-tuple-element.26), channel_id=1, source_target_pairs={{0,16},{1,19},{2,18},{3,17},{16,0},{17,3},{18,2},{19,1},{4,20},{5,... | collective-permute-start | bytes 442376 | tf_op jit(solution)/shard_map/ppermute | solution.py:267
  82.2 3.7 %collective-permute-done.3.refs_6_ = bf16[2,2,72,256]{3,2,1,0:T(8,128)(2,1)S(1)} collective-permute-done((bf16[2,2,72,256]{3,2,1,0:T(8,128)(2,1)S(1)}, bf16[2,2,72,256]{3,2,1,0:T(8,128)(2,1)S(1)}, u32[]{:S(2)}, u32[]{:S(2)}) %collective-permute-start.3) | collective-permute-done | bytes 147488 | tf_op jit(solution)/shard_map/ppermute | solution.py:267
  85.9 1.5 %finish.1 = bf16[512,128]{1,0:T(8,128)(2,1)} custom-call(s32[2]{0:T(128)S(1)} %pad_add_fusion.place_ref, f32[2,64,256]{2,1,0:T(8,128)S(1)} %get-tuple-element.18.refs_0_, f32[2,8,128]{2,1,0:T(8,128)S(1)} %get-tuple-element.19.refs_1_, bf16[2,64,128]{2,1,0:T(8,128)(2,1)S(1)} %get-tuple-element.20.refs_2_, f32[2,64,256]{2,1,0:T(8,128)S(1)} %get-tuple-element.23.refs_3_, ...), custom_call_target="tpu_custom_call" | custom-call | tf_op jit(solution)/shard_map/finish/pallas_call | solution.py:229
Async XLA Ops:
  6.5 7.3 %copy-start = (bf16[72,256]{1,0:T(8,128)(2,1)S(1)}, bf16[72,256]{1,0:T(8,128)(2,1)}, u32[]{:S(2)}) copy-start(bf16[72,256]{1,0:T(8,128)(2,1)} %get-tuple-element.16) | copy-start | bytes 110596
  6.5 68.5 %all-to-all-start = ((bf16[8,4,256,256]{3,2,1,0:T(8,128)(2,1)}), bf16[8,4,256,256]{3,2,1,0:T(8,128)(2,1)}, u32[]{:S(2)}, u32[]{:S(2)}) async-start(bf16[8,4,256,256]{3,2,1,0:T(8,128)(2,1)} %get-tuple-element.17), calls=%async_computation | async-start | bytes 8388608 | tf_op jit(solution)/shard_map/all_to_all | solution.py:260
  48.7 21.7 %collective-permute-start.1 = (bf16[16,72,256]{2,1,0:T(8,128)(2,1)S(1)}, bf16[16,72,256]{2,1,0:T(8,128)(2,1)S(1)}, u32[]{:S(2)}, u32[]{:S(2)}) collective-permute-start(bf16[16,72,256]{2,1,0:T(8,128)(2,1)S(1)} %bitcast.6), channel_id=1, source_target_pairs={{0,2},{2,0},{1,3},{3,1},{4,6},{6,4},{5,7},{7,5},{8,10},{10,8},{9,1... | collective-permute-start | bytes 1769480 | tf_op jit(solution)/shard_map/ppermute | solution.py:262
  51.1 23.8 %collective-permute-start = (bf16[16,72,256]{2,1,0:T(8,128)(2,1)S(1)}, bf16[16,72,256]{2,1,0:T(8,128)(2,1)S(1)}, u32[]{:S(2)}, u32[]{:S(2)}) collective-permute-start(bf16[16,72,256]{2,1,0:T(8,128)(2,1)S(1)} %bitcast.7), channel_id=1, source_target_pairs={{0,1},{1,0},{2,3},{3,2},{4,5},{5,4},{6,7},{7,6},{8,9},{9,8},{10,11... | collective-permute-start | bytes 1769480 | tf_op jit(solution)/shard_map/ppermute | solution.py:263
  70.3 7.2 %collective-permute-start.2 = (bf16[16,72,256]{2,1,0:T(8,128)(2,1)S(1)}, bf16[16,72,256]{2,1,0:T(8,128)(2,1)S(1)}, u32[]{:S(2)}, u32[]{:S(2)}) collective-permute-start(bf16[16,72,256]{2,1,0:T(8,128)(2,1)S(1)} %collective-permute-done.1.own_a_ref), channel_id=1, source_target_pairs={{0,1},{1,0},{2,3},{3,2},{4,5},{5,4},{6,7},{7,6},{8,9},{9,8},{10,11... | collective-permute-start | bytes 1769480 | tf_op jit(solution)/shard_map/ppermute | solution.py:264
  78.8 7.1 %collective-permute-start.3 = (bf16[2,2,72,256]{3,2,1,0:T(8,128)(2,1)S(1)}, bf16[2,2,72,256]{3,2,1,0:T(8,128)(2,1)S(1)}, u32[]{:S(2)}, u32[]{:S(2)}) collective-permute-start(bf16[2,2,72,256]{3,2,1,0:T(8,128)(2,1)S(1)} %get-tuple-element.26), channel_id=1, source_target_pairs={{0,16},{1,19},{2,18},{3,17},{16,0},{17,3},{18,2},{19,1},{4,20},{5,... | collective-permute-start | bytes 442376 | tf_op jit(solution)/shard_map/ppermute | solution.py:267

commit v4 on v3

v4 whole, which is shorter than its diff:
```python
import jax
import jax.numpy as jnp
from jax import lax
from jax.experimental import pallas as pl
from jax.experimental.pallas import tpu as pltpu
from jax.sharding import Mesh, PartitionSpec as P

D = 8192
LIVE = 64
ROWS = 128
FEATS = 256
EXTRA = 8
BLOCK_ROWS = LIVE + EXTRA
EARLY = 48
LATE = LIVE - EARLY
NEAR = LIVE + EARLY
AXES = ("zh", "zl", "yl", "x", "yh", "c")
BF = jnp.bfloat16
F32 = jnp.float32
VMEM_BYTES = 24 * 1024 * 1024


def split3(value):
    hi = value.astype(BF).astype(F32)
    mid = (value - hi).astype(BF).astype(F32)
    lo = (value - hi - mid).astype(BF).astype(F32)
    return hi, mid, lo


def diagonal(size):
    return lax.broadcasted_iota(jnp.int32, (size, size), 0) == lax.broadcasted_iota(jnp.int32, (size, size), 1)


def slot_table(live):
    rows = lax.broadcasted_iota(jnp.int32, (ROWS, ROWS), 0)
    cols = lax.broadcasted_iota(jnp.int32, (ROWS, ROWS), 1)
    before = jnp.where(rows <= cols, 1.0, 0.0).astype(BF)
    wide = jnp.broadcast_to(live, (16, ROWS))
    rank = jnp.dot(wide.astype(BF), before, preferred_element_type=F32)[0:1, :]
    slot = lax.broadcasted_iota(jnp.int32, (LIVE, ROWS), 0).astype(F32) + 1.0
    return jnp.where((slot == rank) & (live > 0.5), 1.0, 0.0)


def compact_kernel(stream_ref, gain_ref, live_ref, block_ref, early_ref):
    stream = stream_ref[...]
    live = live_ref[...].astype(F32)
    table = slot_table(live)
    scaled = (stream * gain_ref[...]).astype(BF)
    rows = jnp.dot(table.astype(BF), scaled, preferred_element_type=F32).astype(BF)
    block_ref[0:LIVE, :] = rows
    early_ref[0:EARLY, :] = rows[0:EARLY, :]
    square = jnp.sum(stream * stream, axis=1, keepdims=True)
    square_row = jnp.sum(jnp.where(diagonal(ROWS), square, 0.0), axis=0, keepdims=True)
    hi, mid, lo = split3(square_row)
    index = lax.broadcasted_iota(jnp.int32, (EXTRA, ROWS), 0)
    for ref, start, first in ((block_ref, LIVE, 0), (early_ref, EARLY, 2)):
        ref[start:, 0:ROWS] = jnp.where(index == first, live, jnp.where(index == first + 1, mid, 0.0)).astype(BF)
        ref[start:, ROWS:] = jnp.where(index == first, hi, jnp.where(index == first + 1, lo, 0.0)).astype(BF)


def compact(stream, gain, live):
    return pl.pallas_call(
        compact_kernel,
        out_shape=[
            jax.ShapeDtypeStruct((BLOCK_ROWS, FEATS), BF),
            jax.ShapeDtypeStruct((EARLY + EXTRA, FEATS), BF),
        ],
        name="compact",
    )(stream, gain.reshape(1, FEATS), live.reshape(1, ROWS))


def join(block, early):
    return jnp.concatenate([block[:LIVE], early[:EARLY], block[LIVE:] + early[EARLY:]], axis=0)


def restore(master):
    tile = master.T.reshape(4, 32, 128)
    size = jnp.abs(tile)
    largest = jnp.max(size, axis=1, keepdims=True)
    wide = largest * 8388609.0
    power = jnp.abs(wide - wide * (1.0 - 2.0**-24))
    power = jnp.where(power > largest, power * 0.5, power)
    power = jnp.where(power * 2.0 <= largest, power * 2.0, power)
    scale = jnp.clip(power, 2.0**-32, 2.0**4) * 0.25
    level = jnp.zeros_like(size)
    for edge, value in ((0.25, 0.5), (0.75, 1.0), (1.25, 1.5), (1.75, 2.0), (2.5, 3.0), (3.5, 4.0), (5.0, 6.0)):
        level = jnp.where(size >= scale * edge, scale * value, level)
    return jnp.where(tile < 0.0, -level, level).reshape(128, 128).T.astype(BF)


def pack_kernel(gate_hbm, up_hbm, out_hbm, gate_ref, up_ref, packed_ref, in_sems, out_sems):
    loads = []
    for zl in range(4):
        rows = pl.ds(zl * 2 * FEATS, 2 * FEATS)
        for side, (hbm, ref) in enumerate(((gate_hbm, gate_ref), (up_hbm, up_ref))):
            load = pltpu.make_async_copy(hbm.at[rows, :], ref.at[rows, :], in_sems.at[zl, side])
            load.start()
            loads.append(load)
    stores = []
    for zl in range(4):
        loads[2 * zl].wait()
        loads[2 * zl + 1].wait()
        for yl in range(2):
            for side, ref in enumerate((gate_ref, up_ref)):
                for tile in range(2):
                    first = (2 * zl + yl) * FEATS + tile * 128
                    value = restore(ref[first : first + 128, :])
                    packed_ref[yl, zl, tile * 128 : (tile + 1) * 128, side * 128 : (side + 1) * 128] = value
            for x in range(4):
                store = pltpu.make_async_copy(packed_ref.at[yl, zl], out_hbm.at[4 * yl + x, zl], out_sems.at[zl, yl, x])
                store.start()
                stores.append(store)
    for store in stores:
        store.wait()


def pack(gate_master, up_master):
    return pl.pallas_call(
        pack_kernel,
        in_specs=[pl.BlockSpec(memory_space=pl.ANY)] * 2,
        out_specs=pl.BlockSpec(memory_space=pl.ANY),
        out_shape=jax.ShapeDtypeStruct((8, 4, FEATS, 256), BF),
        scratch_shapes=[
            pltpu.VMEM((8 * FEATS, 128), F32),
            pltpu.VMEM((8 * FEATS, 128), F32),
            pltpu.VMEM((2, 4, FEATS, 256), BF),
            pltpu.SemaphoreType.DMA((4, 2)),
            pltpu.SemaphoreType.DMA((4, 2, 4)),
        ],
        compiler_params=pltpu.CompilerParams(vmem_limit_bytes=62 * 1024 * 1024),
        name="pack",
    )(gate_master, up_master)


def square_rows(a_ref):
    tails = jnp.sum(a_ref[:, NEAR:, :].astype(F32), axis=0)
    return [tails[t : t + 1, ROWS:] + tails[t + 1 : t + 2, :ROWS] + tails[t + 1 : t + 2, ROWS:] for t in (0, 2)]


def fetch(w_hbm, w_ref, sems, first):
    loads = [pltpu.make_async_copy(w_hbm.at[first + x], w_ref.at[x], sems.at[x]) for x in range(4)]
    for load in loads:
        load.start()
    return loads


def multiply(rows_refs, w_ref, loads):
    own_a_ref, other_a_ref, own_late_ref, other_late_ref = rows_refs
    pieces = ((own_a_ref, NEAR), (own_late_ref, LATE), (other_a_ref, NEAR), (other_late_ref, LATE))
    total = jnp.zeros((4 * LIVE, 256), F32)
    for load in loads:
        load.wait()
    for z in range(16):
        rows = jnp.concatenate([ref[z, 0:count, :] for ref, count in pieces], axis=0)
        total = total + jnp.dot(rows, w_ref[z // 4, z % 4], preferred_element_type=F32)
    return total


def sent_kernel(place_ref, own_a_ref, other_a_ref, own_late_ref, other_late_ref, w_hbm, sent_ref, w_ref, sems):
    yl, yh, c = place_ref[0], place_ref[1], place_ref[2]
    loads = fetch(w_hbm, w_ref, sems, 4 * (1 - yl))
    index = lax.broadcasted_iota(jnp.int32, (EXTRA, ROWS), 0)
    for i, a_ref in enumerate((own_a_ref, other_a_ref)):
        for flip_h, square in enumerate(square_rows(a_ref)):
            hi, mid, lo = split3(square)
            left = jnp.where(index == 1, mid, 0.0)
            right = jnp.where(index == 0, hi, jnp.where(index == 1, lo, 0.0))
            sent_ref[yh ^ flip_h, c ^ i, LIVE:, 0:ROWS] = left.astype(BF)
            sent_ref[yh ^ flip_h, c ^ i, LIVE:, ROWS:] = right.astype(BF)
    total = multiply((own_a_ref, other_a_ref, own_late_ref, other_late_ref), w_ref, loads)
    for i in range(2):
        for flip_h in range(2):
            first = (2 * i + flip_h) * LIVE
            sent_ref[yh ^ flip_h, c ^ i, 0:LIVE, :] = total[first : first + LIVE, :].astype(BF)


def own_kernel(
    place_ref, own_a_ref, other_a_ref, own_late_ref, other_late_ref, w_hbm,
    own_ref, square_ref, table_ref, w_ref, sems,
):
    loads = fetch(w_hbm, w_ref, sems, 4 * place_ref[0])
    total = multiply((own_a_ref, other_a_ref, own_late_ref, other_late_ref), w_ref, loads)
    for i, a_ref in enumerate((own_a_ref, other_a_ref)):
        lives = a_ref[0, NEAR:, :].astype(F32)
        for flip_h, square in enumerate(square_rows(a_ref)):
            square_ref[i, flip_h] = jnp.broadcast_to(square, (EXTRA, ROWS))
            table_ref[i, flip_h] = slot_table(lives[2 * flip_h : 2 * flip_h + 1, :ROWS]).astype(BF)
            first = (2 * i + flip_h) * LIVE
            own_ref[i, flip_h] = total[first : first + LIVE, :]


def partial(kernel, name, place, rows, weights, out_shape):
    vmem = pl.BlockSpec(memory_space=pltpu.VMEM)
    return pl.pallas_call(
        kernel,
        in_specs=[pl.BlockSpec(memory_space=pltpu.SMEM)] + [vmem] * 4 + [pl.BlockSpec(memory_space=pl.ANY)],
        out_specs=[vmem] * len(out_shape),
        out_shape=out_shape,
        scratch_shapes=[pltpu.VMEM((4, 4, FEATS, 256), BF), pltpu.SemaphoreType.DMA((4,))],
        compiler_params=pltpu.CompilerParams(vmem_limit_bytes=VMEM_BYTES),
        name=name,
    )(place, *rows, weights)


SENT_SHAPES = [jax.ShapeDtypeStruct((2, 2, BLOCK_ROWS, 256), BF)]
OWN_SHAPES = [
    jax.ShapeDtypeStruct((2, 2, LIVE, 256), F32),
    jax.ShapeDtypeStruct((2, 2, EXTRA, ROWS), F32),
    jax.ShapeDtypeStruct((2, 2, LIVE, ROWS), BF),
]


def finish_kernel(place_ref, own_ref, square_ref, table_ref, other_ref, out_ref):
    yh, c = place_ref[1], place_ref[2]
    for flip_h in range(2):
        for i in range(2):
            sent = other_ref[yh ^ flip_h, c ^ i].astype(F32)
            rows = own_ref[i, flip_h] + sent[0:LIVE, :]
            tail = sent[LIVE:, :]
            square = square_ref[i, flip_h, 0:1, :] + tail[0:1, ROWS:] + tail[1:2, :ROWS] + tail[1:2, ROWS:]
            table = table_ref[i, flip_h]
            inverse = lax.rsqrt(square * (1.0 / D) + 1e-06)
            rows = rows * jnp.sum(table.astype(F32) * inverse, axis=1, keepdims=True)
            gate, up = rows[:, :128], rows[:, 128:]
            hidden = (gate / (1.0 + jnp.exp(-gate)) * up).astype(BF)
            spread = lax.dot_general(table, hidden, (((0,), (0,)), ((), ())), preferred_element_type=F32)
            block = 2 * (yh ^ flip_h) + (c ^ i)
            out_ref[pl.ds(pl.multiple_of(block * ROWS, ROWS), ROWS), :] = spread.astype(BF)


def finish(place, own, square, table, other):
    return pl.pallas_call(
        finish_kernel,
        in_specs=[pl.BlockSpec(memory_space=pltpu.SMEM)] + [pl.BlockSpec(memory_space=pltpu.VMEM)] * 4,
        out_specs=pl.BlockSpec(memory_space=pltpu.VMEM),
        out_shape=jax.ShapeDtypeStruct((4 * ROWS, 128), BF),
        compiler_params=pltpu.CompilerParams(vmem_limit_bytes=VMEM_BYTES),
        name="finish",
    )(place, own, square, table, other)


def partner_groups():
    return [
        [((yl * 4 + x) * 2 + (h ^ (yl & c))) * 2 + c for yl in range(2) for x in range(4)]
        for h in range(2)
        for c in range(2)
    ]


def partner_moves():
    moves = []
    for yl in range(2):
        for yh in range(2):
            for c in range(2):
                moves.append(((yl * 2 + yh) * 2 + c, ((1 - yl) * 2 + (yh ^ c)) * 2 + c))
    return moves


def shards(gate_master, up_master, stream, norm_gain, live_rows):
    swap = [(0, 1), (1, 0)]
    place = jnp.stack([lax.axis_index(name) for name in ("yl", "yh", "c")]).astype(jnp.int32)
    block, early = compact(stream, norm_gain, live_rows)
    early = lax.ppermute(early, "yh", swap)
    gate_master, block = lax.optimization_barrier((gate_master, block))
    weights = pack(gate_master, up_master)
    early, weights = lax.optimization_barrier((early, weights))
    weights = lax.all_to_all(weights, ("yl", "x", "yh", "c"), 0, 0, axis_index_groups=partner_groups())
    own_a = lax.all_gather(join(block, early), ("zh", "zl"), axis=0, tiled=False)
    own_late = lax.ppermute(own_a[:, EARLY:LIVE, :], "yh", swap)
    own_a, own_late = lax.optimization_barrier((own_a, own_late))
    other_a = lax.ppermute(own_a, "c", swap)
    other_late = lax.ppermute(own_late, "c", swap)
    rows = (own_a, other_a, own_late, other_late)
    (sent,) = partial(sent_kernel, "sent_sums", place, rows, weights, SENT_SHAPES)
    other = lax.ppermute(sent, ("yl", "yh", "c"), partner_moves())
    own, square, table = partial(own_kernel, "own_sums", place, rows, weights, OWN_SHAPES)
    return finish(place, own, square, table, other)


def solution(mesh):
    fine = Mesh(mesh.devices.reshape(4, 4, 2, 4, 2, 2), AXES)
    learner, tp = ("zh", "zl", "yl"), ("yh", "c")
    placed = (
        P("x", learner + tp),
        P("x", learner + tp),
        P(("x",) + tp, learner),
        P(learner),
        P(("x",) + tp),
    )
    return jax.shard_map(shards, mesh=fine, in_specs=placed, out_specs=P("x", learner + tp), check_vma=False)
```

time: 87.8 us -> 85.8 us (0.977)
  waiting for transfers between devices: 15.1 us -> 7.6 us
  blocking collectives: 34.9 us -> 37.1 us
  Pallas kernels: 11.8 us -> 13.8 us
  starting transfers between devices: 25.4 us -> 26.6 us
    ppermute x3 -> x4, waiting for transfers between devices: 11.4 us -> 6.99 us  [the longest x1 5.75 us: shards(): own_late = lax.ppermute(own_a[:, EARLY:LIVE, :], 'yh', swap)]
    ppermute x3 -> x4, starting transfers between devices: 14.8 us -> 18.4 us  [the longest x1 7.61 us: shards(): other_a = lax.ppermute(own_a, 'c', swap)]
    ppermute x1, waiting for transfers between devices: 3.73 us -> 0.61 us  [shards(): other = lax.ppermute(sent, ('yl', 'yh', 'c'), partner_moves())]
    all_to_all x1, starting transfers between devices: 7.31 us -> 4.58 us  [shards(): lax.all_to_all(weights, ('yl', 'x', 'yh', 'c'), 0, 0, axis_index_groups=p...]
    all_gather x1, blocking collectives: 34.9 us -> 37.1 us  [shards(): lax.all_gather(join(block, early), ('zh', 'zl'), axis=0, tiled=False)]
    pallas_call x3 -> x4, Pallas kernels: 10.3 us -> 12.3 us  [the longest x2 5.64 us: partial(): pl.pallas_call(kernel, in_specs=[pl.BlockSpec(memory_space=pltpu.SMEM)] +...]
  transfers between devices with their start and end apart: 5 -> 6, of which waited for: 2 -> 3; matrix products, arithmetic and copies ran while one was open for 0% -> 0% of each run, Pallas kernels for 3% -> 9%
where the time goes in v4:
time: 85.8 us; the launch traced here: 85.4 us
  blocking collectives  37.1 us (43%)
  starting transfers between devices  26.6 us (31%)
  Pallas kernels  13.8 us (16%)
  waiting for transfers between devices  7.6 us (9%)
    all_gather x1, blocking collectives, shards(): lax.all_gather(join(block, early), ('zh', 'zl'), axis=0, tiled=False)  37.1 us
    ppermute x1, starting transfers between devices, shards(): other_a = lax.ppermute(own_a, 'c', swap)  7.61 us
    ppermute x1, waiting for transfers between devices, shards(): own_late = lax.ppermute(own_a[:, EARLY:LIVE, :], 'yh', swap)  5.75 us
    pallas_call x2, Pallas kernels, partial(): pl.pallas_call(kernel, in_specs=[pl.BlockSpec(memory_space=pltpu.SMEM)] +...  5.64 us
    ppermute x1, starting transfers between devices, shards(): early = lax.ppermute(early, 'yh', swap)  5.64 us
    pallas_call x1, Pallas kernels, pack(): pl.pallas_call(pack_kernel, in_specs=[pl.BlockSpec(memory_space=pl.ANY)]...  4.89 us
    all_to_all x1, starting transfers between devices, shards(): lax.all_to_all(weights, ('yl', 'x', 'yh', 'c'), 0, 0, axis_index_groups=p...  4.58 us
    ppermute x1, starting transfers between devices, shards(): other = lax.ppermute(sent, ('yl', 'yh', 'c'), partner_moves())  3.64 us
  transfers between devices with their start and end apart: 6, of which 3 were waited for; matrix products, arithmetic and copies ran while one was open for 0% of the time, Pallas kernels for 9%

profile of v4, /device:TPU:1, one launch (start us, length us, event | category | flops | bytes accessed | tf_op | source)
XLA Modules:
  0.0 85.4 jit_solution(6523417396449331804)
XLA Ops:
  0.0 1.8 %compact.1 = (bf16[72,256]{1,0:T(8,128)(2,1)}, bf16[56,256]{1,0:T(8,128)(2,1)}) custom-call(f32[128,256]{1,0:T(8,128)} %stream_ref.1, f32[1,256]{1,0:T(1,128)} %bitcast.10, s32[1,128]{1,0:T(1,128)} %bitcast.11), custom_call_target="tpu_custom_call" | custom-call | tf_op jit(solution)/shard_map/compact/pallas_call | solution.py:62
  1.8 5.6 %collective-permute-start = (bf16[56,256]{1,0:T(8,128)(2,1)}, bf16[56,256]{1,0:T(8,128)(2,1)S(1)}, u32[]{:S(2)}, u32[]{:S(2)}) collective-permute-start(bf16[56,256]{1,0:T(8,128)(2,1)} %get-tuple-element.18), channel_id=1, source_target_pairs={{0,2},{2,0},{1,3},{3,1},{4,6},{6,4},{5,7},{7,5},{8,10},{10,8},{9,1... | collective-permute-start | bytes 86024 | tf_op jit(solution)/shard_map/ppermute | solution.py:263
  7.5 4.9 %pack.1 = bf16[8,4,256,256]{3,2,1,0:T(8,128)(2,1)} custom-call(f32[2048,128]{1,0:T(8,128)} %gate_hbm, f32[2048,128]{1,0:T(8,128)} %up_hbm.1), custom_call_target="tpu_custom_call" | custom-call | tf_op jit(solution)/shard_map/pack/pallas_call | solution.py:118
  12.4 0.0 copy-start
  12.4 0.0 collective-permute-done
  12.4 4.6 %all-to-all-start = ((bf16[8,4,256,256]{3,2,1,0:T(8,128)(2,1)}), bf16[8,4,256,256]{3,2,1,0:T(8,128)(2,1)}, u32[]{:S(2)}, u32[]{:S(2)}) async-start(bf16[8,4,256,256]{3,2,1,0:T(8,128)(2,1)} %pack.1), calls=%async_computation | async-start | bytes 8388608 | tf_op jit(solution)/shard_map/all_to_all | solution.py:267
  17.0 0.0 copy-done
  17.0 37.1 %all-gather = bf16[1920,256]{1,0:T(8,128)(2,1)S(1)} all-gather(bf16[120,256]{1,0:T(8,128)(2,1)S(1)} %pad_maximum_fusion), channel_id=2, replica_groups=mesh['zh'=4,'zl'=4,'yl'=2,'x'=4,'yh'=2,'c'=2] {'zh','zl'}, dimensions={0}, use_global_device_ids=true | all-gather | bytes 1044480 | tf_op jit(solution)/shard_map/all_gather | solution.py:268
  54.1 3.3 %collective-permute-start.1 = (bf16[16,16,256]{2,1,0:T(8,128)(2,1)S(1)}, bf16[16,16,256]{2,1,0:T(8,128)(2,1)S(1)}, u32[]{:S(2)}, u32[]{:S(2)}) collective-permute-start(bf16[16,16,256]{2,1,0:T(8,128)(2,1)S(1)} %slice.20), channel_id=1, source_target_pairs={{0,2},{2,0},{1,3},{3,1},{4,6},{6,4},{5,7},{7,5},{8,10},{10,8},{9,1... | collective-permute-start | bytes 393224 | tf_op jit(solution)/shard_map/ppermute | solution.py:269
  57.4 5.8 %collective-permute-done.1.own_late_ref = bf16[16,16,256]{2,1,0:T(8,128)(2,1)S(1)} collective-permute-done((bf16[16,16,256]{2,1,0:T(8,128)(2,1)S(1)}, bf16[16,16,256]{2,1,0:T(8,128)(2,1)S(1)}, u32[]{:S(2)}, u32[]{:S(2)}) %collective-permute-start.1) | collective-permute-done | bytes 131104 | tf_op jit(solution)/shard_map/ppermute | solution.py:269
  63.1 7.6 %collective-permute-start.2 = (bf16[16,120,256]{2,1,0:T(8,128)(2,1)S(1)}, bf16[16,120,256]{2,1,0:T(8,128)(2,1)S(1)}, u32[]{:S(2)}, u32[]{:S(2)}) collective-permute-start(bf16[16,120,256]{2,1,0:T(8,128)(2,1)S(1)} %bitcast.7), channel_id=1, source_target_pairs={{0,1},{1,0},{2,3},{3,2},{4,5},{5,4},{6,7},{7,6},{8,9},{9,8},{10,11... | collective-permute-start | bytes 2949128 | tf_op jit(solution)/shard_map/ppermute | solution.py:271
  70.7 1.9 %collective-permute-start.3 = (bf16[16,16,256]{2,1,0:T(8,128)(2,1)S(1)}, bf16[16,16,256]{2,1,0:T(8,128)(2,1)S(1)}, u32[]{:S(2)}, u32[]{:S(2)}) collective-permute-start(bf16[16,16,256]{2,1,0:T(8,128)(2,1)S(1)} %collective-permute-done.1.own_late_ref), channel_id=1, source_target_pairs={{0,1},{1,0},{2,3},{3,2},{4,5},{5,4},{6,7},{7,6},{8,9},{9,8},{10,11... | collective-permute-start | bytes 393224 | tf_op jit(solution)/shard_map/ppermute | solution.py:272
  72.7 0.1 pad_add_fusion.place_ref
  72.7 1.2 %collective-permute-done.3.other_late_ref = bf16[16,16,256]{2,1,0:T(8,128)(2,1)S(1)} collective-permute-done((bf16[16,16,256]{2,1,0:T(8,128)(2,1)S(1)}, bf16[16,16,256]{2,1,0:T(8,128)(2,1)S(1)}, u32[]{:S(2)}, u32[]{:S(2)}) %collective-permute-start.3) | collective-permute-done | bytes 131104 | tf_op jit(solution)/shard_map/ppermute | solution.py:272
  74.0 0.0 collective-permute-done.2.other_a_ref
  74.0 0.0 all-to-all-done.w_hbm
  74.0 2.8 %sent_sums.1 = bf16[2,2,72,256]{3,2,1,0:T(8,128)(2,1)S(1)} custom-call(s32[3]{0:T(128)S(1)} %pad_add_fusion.place_ref, bf16[16,120,256]{2,1,0:T(8,128)(2,1)S(1)} %bitcast.8, bf16[16,120,256]{2,1,0:T(8,128)(2,1)S(1)} %collective-permute-done.2.other_a_ref, bf16[16,16,256]{2,1,0:T(8,128)(2,1)S(1)} %collective-permute-done.1.own_late_ref, ...), custom_call_target="tpu_custom_call" | custom-call | tf_op jit(solution)/shard_map/sent_sums/pallas_call | solution.py:194
  76.8 3.6 %collective-permute-start.4 = (bf16[2,2,72,256]{3,2,1,0:T(8,128)(2,1)S(1)}, bf16[2,2,72,256]{3,2,1,0:T(8,128)(2,1)S(1)}, u32[]{:S(2)}, u32[]{:S(2)}) collective-permute-start(bf16[2,2,72,256]{3,2,1,0:T(8,128)(2,1)S(1)} %sent_sums.1), channel_id=1, source_target_pairs={{0,16},{1,19},{2,18},{3,17},{16,0},{17,3},{18,2},{19,1},{4,20},{5,... | collective-permute-start | bytes 442376 | tf_op jit(solution)/shard_map/ppermute | solution.py:275
  80.4 2.8 %own_sums.1 = (f32[2,2,64,256]{3,2,1,0:T(8,128)S(1)}, f32[2,2,8,128]{3,2,1,0:T(8,128)S(1)}, bf16[2,2,64,128]{3,2,1,0:T(8,128)(2,1)S(1)}) custom-call(s32[3]{0:T(128)S(1)} %pad_add_fusion.place_ref, bf16[16,120,256]{2,1,0:T(8,128)(2,1)S(1)} %bitcast.9, bf16[16,120,256]{2,1,0:T(8,128)(2,1)S(1)} %collective-permute-done.2.other_a_ref, ...), custom_call_target="tpu_custom_call" | custom-call | tf_op jit(solution)/shard_map/own_sums/pallas_call | solution.py:194
  83.3 0.6 collective-permute-done.4.other_ref
  83.9 1.5 %finish.1 = bf16[512,128]{1,0:T(8,128)(2,1)} custom-call(s32[3]{0:T(128)S(1)} %pad_add_fusion.place_ref, f32[2,2,64,256]{3,2,1,0:T(8,128)S(1)} %get-tuple-element.24.own_ref, f32[2,2,8,128]{3,2,1,0:T(8,128)S(1)} %get-tuple-element.25.square_ref, bf16[2,2,64,128]{3,2,1,0:T(8,128)(2,1)S(1)} %get-tuple-element.26.table_ref, ...), custom_call_target="tpu_custom_call" | custom-call | tf_op jit(solution)/shard_map/finish/pallas_call | solution.py:232
  (5 shorter events, 0.0 us)
Async XLA Ops:
  1.8 10.6 %collective-permute-start = (bf16[56,256]{1,0:T(8,128)(2,1)}, bf16[56,256]{1,0:T(8,128)(2,1)S(1)}, u32[]{:S(2)}, u32[]{:S(2)}) collective-permute-start(bf16[56,256]{1,0:T(8,128)(2,1)} %get-tuple-element.18), channel_id=1, source_target_pairs={{0,2},{2,0},{1,3},{3,1},{4,6},{6,4},{5,7},{7,5},{8,10},{10,8},{9,1... | collective-permute-start | bytes 86024 | tf_op jit(solution)/shard_map/ppermute | solution.py:263
  12.4 4.6 %copy-start = (bf16[72,256]{1,0:T(8,128)(2,1)S(1)}, bf16[72,256]{1,0:T(8,128)(2,1)}, u32[]{:S(2)}) copy-start(bf16[72,256]{1,0:T(8,128)(2,1)} %get-tuple-element.17) | copy-start | bytes 110596
  12.4 61.6 %all-to-all-start = ((bf16[8,4,256,256]{3,2,1,0:T(8,128)(2,1)}), bf16[8,4,256,256]{3,2,1,0:T(8,128)(2,1)}, u32[]{:S(2)}, u32[]{:S(2)}) async-start(bf16[8,4,256,256]{3,2,1,0:T(8,128)(2,1)} %pack.1), calls=%async_computation | async-start | bytes 8388608 | tf_op jit(solution)/shard_map/all_to_all | solution.py:267
  54.1 9.0 %collective-permute-start.1 = (bf16[16,16,256]{2,1,0:T(8,128)(2,1)S(1)}, bf16[16,16,256]{2,1,0:T(8,128)(2,1)S(1)}, u32[]{:S(2)}, u32[]{:S(2)}) collective-permute-start(bf16[16,16,256]{2,1,0:T(8,128)(2,1)S(1)} %slice.20), channel_id=1, source_target_pairs={{0,2},{2,0},{1,3},{3,1},{4,6},{6,4},{5,7},{7,5},{8,10},{10,8},{9,1... | collective-permute-start | bytes 393224 | tf_op jit(solution)/shard_map/ppermute | solution.py:269
  63.1 10.9 %collective-permute-start.2 = (bf16[16,120,256]{2,1,0:T(8,128)(2,1)S(1)}, bf16[16,120,256]{2,1,0:T(8,128)(2,1)S(1)}, u32[]{:S(2)}, u32[]{:S(2)}) collective-permute-start(bf16[16,120,256]{2,1,0:T(8,128)(2,1)S(1)} %bitcast.7), channel_id=1, source_target_pairs={{0,1},{1,0},{2,3},{3,2},{4,5},{5,4},{6,7},{7,6},{8,9},{9,8},{10,11... | collective-permute-start | bytes 2949128 | tf_op jit(solution)/shard_map/ppermute | solution.py:271
  70.7 3.2 %collective-permute-start.3 = (bf16[16,16,256]{2,1,0:T(8,128)(2,1)S(1)}, bf16[16,16,256]{2,1,0:T(8,128)(2,1)S(1)}, u32[]{:S(2)}, u32[]{:S(2)}) collective-permute-start(bf16[16,16,256]{2,1,0:T(8,128)(2,1)S(1)} %collective-permute-done.1.own_late_ref), channel_id=1, source_target_pairs={{0,1},{1,0},{2,3},{3,2},{4,5},{5,4},{6,7},{7,6},{8,9},{9,8},{10,11... | collective-permute-start | bytes 393224 | tf_op jit(solution)/shard_map/ppermute | solution.py:272
  76.8 7.1 %collective-permute-start.4 = (bf16[2,2,72,256]{3,2,1,0:T(8,128)(2,1)S(1)}, bf16[2,2,72,256]{3,2,1,0:T(8,128)(2,1)S(1)}, u32[]{:S(2)}, u32[]{:S(2)}) collective-permute-start(bf16[2,2,72,256]{3,2,1,0:T(8,128)(2,1)S(1)} %sent_sums.1), channel_id=1, source_target_pairs={{0,16},{1,19},{2,18},{3,17},{16,0},{17,3},{18,2},{19,1},{4,20},{5,... | collective-permute-start | bytes 442376 | tf_op jit(solution)/shard_map/ppermute | solution.py:275

commit v5 on v4

--- a/solution.py
+++ b/solution.py
@@ -73,19 +73,25 @@
     return jnp.concatenate([block[:LIVE], early[:EARLY], block[LIVE:] + early[EARLY:]], axis=0)
 
 
+def power_below(value):
+    wide = value * 8388609.0
+    return jnp.abs(wide - wide * (1.0 - 2.0**-24))
+
+
 def restore(master):
     tile = master.T.reshape(4, 32, 128)
     size = jnp.abs(tile)
     largest = jnp.max(size, axis=1, keepdims=True)
-    wide = largest * 8388609.0
-    power = jnp.abs(wide - wide * (1.0 - 2.0**-24))
+    power = power_below(largest)
     power = jnp.where(power > largest, power * 0.5, power)
     power = jnp.where(power * 2.0 <= largest, power * 2.0, power)
     scale = jnp.clip(power, 2.0**-32, 2.0**4) * 0.25
-    level = jnp.zeros_like(size)
-    for edge, value in ((0.25, 0.5), (0.75, 1.0), (1.25, 1.5), (1.75, 2.0), (2.5, 3.0), (3.5, 4.0), (5.0, 6.0)):
-        level = jnp.where(size >= scale * edge, scale * value, level)
-    return jnp.where(tile < 0.0, -level, level).reshape(128, 128).T.astype(BF)
+    inverse = power_below((4.0 / scale) * (1.0 + 2.0**-10))
+    quarters = jnp.floor(size * inverse)
+    step = jnp.where(quarters < 8.0, 1.5 * 2.0**24, jnp.where(quarters < 16.0, 1.5 * 2.0**25, 1.5 * 2.0**26))
+    level = jnp.minimum((quarters + 0.5 + step) - step, 24.0)
+    quarter = scale * 0.25
+    return (level * jnp.where(tile < 0.0, -quarter, quarter)).reshape(128, 128).T.astype(BF)
 
 
 def pack_kernel(gate_hbm, up_hbm, out_hbm, gate_ref, up_ref, packed_ref, in_sems, out_sems):
@@ -266,10 +272,10 @@
     early, weights = lax.optimization_barrier((early, weights))
     weights = lax.all_to_all(weights, ("yl", "x", "yh", "c"), 0, 0, axis_index_groups=partner_groups())
     own_a = lax.all_gather(join(block, early), ("zh", "zl"), axis=0, tiled=False)
-    own_late = lax.ppermute(own_a[:, EARLY:LIVE, :], "yh", swap)
-    own_a, own_late = lax.optimization_barrier((own_a, own_late))
+    late = own_a[:, EARLY:LIVE, :]
+    own_late = lax.ppermute(late, "yh", swap)
+    other_late = lax.ppermute(late, ("yh", "c"), [(0, 3), (1, 2), (2, 1), (3, 0)])
     other_a = lax.ppermute(own_a, "c", swap)
-    other_late = lax.ppermute(own_late, "c", swap)
     rows = (own_a, other_a, own_late, other_late)
     (sent,) = partial(sent_kernel, "sent_sums", place, rows, weights, SENT_SHAPES)
     other = lax.ppermute(sent, ("yl", "yh", "c"), partner_moves())

time: 85.8 us -> 84.4 us (0.984)
  waiting for transfers between devices: 7.6 us -> 4.44 us
  starting transfers between devices: 26.6 us -> 28.7 us
    ppermute x2, waiting for transfers between devices: 6.98 us -> 4.43 us  [the longest x1 2.59 us: shards(): own_late = lax.ppermute(late, 'yh', swap)]
    ppermute x2, starting transfers between devices: 5.18 us -> 6.68 us  [the longest x1 3.45 us: shards(): own_late = lax.ppermute(late, 'yh', swap)]
  transfers between devices with their start and end apart: 6 -> 6, of which waited for: 3 -> 2; matrix products, arithmetic and copies ran while one was open for 0% -> 0% of each run, Pallas kernels for 9% -> 9%
where the time goes in v5:
time: 84.4 us; the launch traced here: 83.9 us
  blocking collectives  37.1 us (44%)
  starting transfers between devices  28.7 us (34%)
  Pallas kernels  13.4 us (16%)
  waiting for transfers between devices  4.44 us (5%)
    all_gather x1, blocking collectives, shards(): lax.all_gather(join(block, early), ('zh', 'zl'), axis=0, tiled=False)  37.1 us
    ppermute x1, starting transfers between devices, shards(): other_a = lax.ppermute(own_a, 'c', swap)  7.3 us
    pallas_call x2, Pallas kernels, partial(): pl.pallas_call(kernel, in_specs=[pl.BlockSpec(memory_space=pltpu.SMEM)] +...  5.64 us
    ppermute x1, starting transfers between devices, shards(): early = lax.ppermute(early, 'yh', swap)  5.64 us
    all_to_all x1, starting transfers between devices, shards(): lax.all_to_all(weights, ('yl', 'x', 'yh', 'c'), 0, 0, axis_index_groups=p...  4.58 us
    pallas_call x1, Pallas kernels, pack(): pl.pallas_call(pack_kernel, in_specs=[pl.BlockSpec(memory_space=pl.ANY)]...  4.48 us
    ppermute x1, starting transfers between devices, shards(): other = lax.ppermute(sent, ('yl', 'yh', 'c'), partner_moves())  4.48 us
    ppermute x1, starting transfers between devices, shards(): own_late = lax.ppermute(late, 'yh', swap)  3.45 us
  transfers between devices with their start and end apart: 6, of which 2 were waited for; matrix products, arithmetic and copies ran while one was open for 0% of the time, Pallas kernels for 9%

profile of v5, /device:TPU:1, one launch (start us, length us, event | category | flops | bytes accessed | tf_op | source)
XLA Modules:
  0.0 83.9 jit_solution(7118503302289346982)
XLA Ops:
  0.0 1.8 %compact.1 = (bf16[72,256]{1,0:T(8,128)(2,1)}, bf16[56,256]{1,0:T(8,128)(2,1)}) custom-call(f32[128,256]{1,0:T(8,128)} %stream_ref.1, f32[1,256]{1,0:T(1,128)} %bitcast.10, s32[1,128]{1,0:T(1,128)} %bitcast.11), custom_call_target="tpu_custom_call" | custom-call | tf_op jit(solution)/shard_map/compact/pallas_call | solution.py:62
  1.8 5.6 %collective-permute-start = (bf16[56,256]{1,0:T(8,128)(2,1)}, bf16[56,256]{1,0:T(8,128)(2,1)S(1)}, u32[]{:S(2)}, u32[]{:S(2)}) collective-permute-start(bf16[56,256]{1,0:T(8,128)(2,1)} %get-tuple-element.16), channel_id=1, source_target_pairs={{0,2},{2,0},{1,3},{3,1},{4,6},{6,4},{5,7},{7,5},{8,10},{10,8},{9,1... | collective-permute-start | bytes 86024 | tf_op jit(solution)/shard_map/ppermute | solution.py:269
  7.5 4.5 %pack.1 = bf16[8,4,256,256]{3,2,1,0:T(8,128)(2,1)} custom-call(f32[2048,128]{1,0:T(8,128)} %gate_hbm, f32[2048,128]{1,0:T(8,128)} %up_hbm.1), custom_call_target="tpu_custom_call" | custom-call | tf_op jit(solution)/shard_map/pack/pallas_call | solution.py:124
  11.9 0.0 copy-start
  12.0 0.0 collective-permute-done
  12.0 4.6 %all-to-all-start = ((bf16[8,4,256,256]{3,2,1,0:T(8,128)(2,1)}), bf16[8,4,256,256]{3,2,1,0:T(8,128)(2,1)}, u32[]{:S(2)}, u32[]{:S(2)}) async-start(bf16[8,4,256,256]{3,2,1,0:T(8,128)(2,1)} %pack.1), calls=%async_computation | async-start | bytes 8388608 | tf_op jit(solution)/shard_map/all_to_all | solution.py:273
  16.6 0.0 copy-done
  16.6 37.1 %all-gather = bf16[1920,256]{1,0:T(8,128)(2,1)S(1)} all-gather(bf16[120,256]{1,0:T(8,128)(2,1)S(1)} %pad_maximum_fusion), channel_id=2, replica_groups=mesh['zh'=4,'zl'=4,'yl'=2,'x'=4,'yh'=2,'c'=2] {'zh','zl'}, dimensions={0}, use_global_device_ids=true | all-gather | bytes 1044480 | tf_op jit(solution)/shard_map/all_gather | solution.py:274
  53.7 7.3 %collective-permute-start.1 = (bf16[16,120,256]{2,1,0:T(8,128)(2,1)S(1)}, bf16[16,120,256]{2,1,0:T(8,128)(2,1)S(1)}, u32[]{:S(2)}, u32[]{:S(2)}) collective-permute-start(bf16[16,120,256]{2,1,0:T(8,128)(2,1)S(1)} %bitcast.6), channel_id=1, source_target_pairs={{0,1},{1,0},{2,3},{3,2},{4,5},{5,4},{6,7},{7,6},{8,9},{9,8},{10,11... | collective-permute-start | bytes 2949128 | tf_op jit(solution)/shard_map/ppermute | solution.py:278
  61.0 3.2 %collective-permute-start.3 = (bf16[16,16,256]{2,1,0:T(8,128)(2,1)S(1)}, bf16[16,16,256]{2,1,0:T(8,128)(2,1)S(1)}, u32[]{:S(2)}, u32[]{:S(2)}) collective-permute-start(bf16[16,16,256]{2,1,0:T(8,128)(2,1)S(1)} %slice.20), channel_id=1, source_target_pairs={{0,3},{1,2},{2,1},{3,0},{4,7},{5,6},{6,5},{7,4},{8,11},{9,10},{10,... | collective-permute-start | bytes 393224 | tf_op jit(solution)/shard_map/ppermute | solution.py:277
  64.2 3.4 %collective-permute-start.2 = (bf16[16,16,256]{2,1,0:T(8,128)(2,1)S(1)}, bf16[16,16,256]{2,1,0:T(8,128)(2,1)S(1)}, u32[]{:S(2)}, u32[]{:S(2)}) collective-permute-start(bf16[16,16,256]{2,1,0:T(8,128)(2,1)S(1)} %slice.20), channel_id=1, source_target_pairs={{0,2},{2,0},{1,3},{3,1},{4,6},{6,4},{5,7},{7,5},{8,10},{10,8},{9,1... | collective-permute-start | bytes 393224 | tf_op jit(solution)/shard_map/ppermute | solution.py:276
  67.7 0.1 pad_add_fusion.place_ref
  67.8 1.8 %collective-permute-done.3.other_late_ref = bf16[16,16,256]{2,1,0:T(8,128)(2,1)S(1)} collective-permute-done((bf16[16,16,256]{2,1,0:T(8,128)(2,1)S(1)}, bf16[16,16,256]{2,1,0:T(8,128)(2,1)S(1)}, u32[]{:S(2)}, u32[]{:S(2)}) %collective-permute-start.3) | collective-permute-done | bytes 131104 | tf_op jit(solution)/shard_map/ppermute | solution.py:277
  69.6 2.6 %collective-permute-done.2.own_late_ref = bf16[16,16,256]{2,1,0:T(8,128)(2,1)S(1)} collective-permute-done((bf16[16,16,256]{2,1,0:T(8,128)(2,1)S(1)}, bf16[16,16,256]{2,1,0:T(8,128)(2,1)S(1)}, u32[]{:S(2)}, u32[]{:S(2)}) %collective-permute-start.2) | collective-permute-done | bytes 131104 | tf_op jit(solution)/shard_map/ppermute | solution.py:276
  72.2 0.0 collective-permute-done.1.other_a_ref
  72.2 0.0 all-to-all-done.w_hbm
  72.2 2.8 %sent_sums.1 = bf16[2,2,72,256]{3,2,1,0:T(8,128)(2,1)S(1)} custom-call(s32[3]{0:T(128)S(1)} %pad_add_fusion.place_ref, bf16[16,120,256]{2,1,0:T(8,128)(2,1)S(1)} %bitcast.8, bf16[16,120,256]{2,1,0:T(8,128)(2,1)S(1)} %collective-permute-done.1.other_a_ref, bf16[16,16,256]{2,1,0:T(8,128)(2,1)S(1)} %collective-permute-done.2.own_late_ref, ...), custom_call_target="tpu_custom_call" | custom-call | tf_op jit(solution)/shard_map/sent_sums/pallas_call | solution.py:200
  75.0 4.5 %collective-permute-start.4 = (bf16[2,2,72,256]{3,2,1,0:T(8,128)(2,1)S(1)}, bf16[2,2,72,256]{3,2,1,0:T(8,128)(2,1)S(1)}, u32[]{:S(2)}, u32[]{:S(2)}) collective-permute-start(bf16[2,2,72,256]{3,2,1,0:T(8,128)(2,1)S(1)} %sent_sums.1), channel_id=1, source_target_pairs={{0,16},{1,19},{2,18},{3,17},{16,0},{17,3},{18,2},{19,1},{4,20},{5,... | collective-permute-start | bytes 442376 | tf_op jit(solution)/shard_map/ppermute | solution.py:281
  79.5 2.8 %own_sums.1 = (f32[2,2,64,256]{3,2,1,0:T(8,128)S(1)}, f32[2,2,8,128]{3,2,1,0:T(8,128)S(1)}, bf16[2,2,64,128]{3,2,1,0:T(8,128)(2,1)S(1)}) custom-call(s32[3]{0:T(128)S(1)} %pad_add_fusion.place_ref, bf16[16,120,256]{2,1,0:T(8,128)(2,1)S(1)} %bitcast.9, bf16[16,120,256]{2,1,0:T(8,128)(2,1)S(1)} %collective-permute-done.1.other_a_ref, ...), custom_call_target="tpu_custom_call" | custom-call | tf_op jit(solution)/shard_map/own_sums/pallas_call | solution.py:200
  82.4 0.0 collective-permute-done.4.other_ref
  82.4 1.5 %finish.1 = bf16[512,128]{1,0:T(8,128)(2,1)} custom-call(s32[3]{0:T(128)S(1)} %pad_add_fusion.place_ref, f32[2,2,64,256]{3,2,1,0:T(8,128)S(1)} %get-tuple-element.20.own_ref, f32[2,2,8,128]{3,2,1,0:T(8,128)S(1)} %get-tuple-element.21.square_ref, bf16[2,2,64,128]{3,2,1,0:T(8,128)(2,1)S(1)} %get-tuple-element.22.table_ref, ...), custom_call_target="tpu_custom_call" | custom-call | tf_op jit(solution)/shard_map/finish/pallas_call | solution.py:238
  (5 shorter events, 0.0 us)
Async XLA Ops:
  1.8 10.2 %collective-permute-start = (bf16[56,256]{1,0:T(8,128)(2,1)}, bf16[56,256]{1,0:T(8,128)(2,1)S(1)}, u32[]{:S(2)}, u32[]{:S(2)}) collective-permute-start(bf16[56,256]{1,0:T(8,128)(2,1)} %get-tuple-element.16), channel_id=1, source_target_pairs={{0,2},{2,0},{1,3},{3,1},{4,6},{6,4},{5,7},{7,5},{8,10},{10,8},{9,1... | collective-permute-start | bytes 86024 | tf_op jit(solution)/shard_map/ppermute | solution.py:269
  11.9 4.6 %copy-start = (bf16[72,256]{1,0:T(8,128)(2,1)S(1)}, bf16[72,256]{1,0:T(8,128)(2,1)}, u32[]{:S(2)}) copy-start(bf16[72,256]{1,0:T(8,128)(2,1)} %get-tuple-element.15) | copy-start | bytes 110596
  12.0 60.3 %all-to-all-start = ((bf16[8,4,256,256]{3,2,1,0:T(8,128)(2,1)}), bf16[8,4,256,256]{3,2,1,0:T(8,128)(2,1)}, u32[]{:S(2)}, u32[]{:S(2)}) async-start(bf16[8,4,256,256]{3,2,1,0:T(8,128)(2,1)} %pack.1), calls=%async_computation | async-start | bytes 8388608 | tf_op jit(solution)/shard_map/all_to_all | solution.py:273
  53.7 18.5 %collective-permute-start.1 = (bf16[16,120,256]{2,1,0:T(8,128)(2,1)S(1)}, bf16[16,120,256]{2,1,0:T(8,128)(2,1)S(1)}, u32[]{:S(2)}, u32[]{:S(2)}) collective-permute-start(bf16[16,120,256]{2,1,0:T(8,128)(2,1)S(1)} %bitcast.6), channel_id=1, source_target_pairs={{0,1},{1,0},{2,3},{3,2},{4,5},{5,4},{6,7},{7,6},{8,9},{9,8},{10,11... | collective-permute-start | bytes 2949128 | tf_op jit(solution)/shard_map/ppermute | solution.py:278
  61.0 8.6 %collective-permute-start.3 = (bf16[16,16,256]{2,1,0:T(8,128)(2,1)S(1)}, bf16[16,16,256]{2,1,0:T(8,128)(2,1)S(1)}, u32[]{:S(2)}, u32[]{:S(2)}) collective-permute-start(bf16[16,16,256]{2,1,0:T(8,128)(2,1)S(1)} %slice.20), channel_id=1, source_target_pairs={{0,3},{1,2},{2,1},{3,0},{4,7},{5,6},{6,5},{7,4},{8,11},{9,10},{10,... | collective-permute-start | bytes 393224 | tf_op jit(solution)/shard_map/ppermute | solution.py:277
  64.2 8.0 %collective-permute-start.2 = (bf16[16,16,256]{2,1,0:T(8,128)(2,1)S(1)}, bf16[16,16,256]{2,1,0:T(8,128)(2,1)S(1)}, u32[]{:S(2)}, u32[]{:S(2)}) collective-permute-start(bf16[16,16,256]{2,1,0:T(8,128)(2,1)S(1)} %slice.20), channel_id=1, source_target_pairs={{0,2},{2,0},{1,3},{3,1},{4,6},{6,4},{5,7},{7,5},{8,10},{10,8},{9,1... | collective-permute-start | bytes 393224 | tf_op jit(solution)/shard_map/ppermute | solution.py:276
  75.0 7.3 %collective-permute-start.4 = (bf16[2,2,72,256]{3,2,1,0:T(8,128)(2,1)S(1)}, bf16[2,2,72,256]{3,2,1,0:T(8,128)(2,1)S(1)}, u32[]{:S(2)}, u32[]{:S(2)}) collective-permute-start(bf16[2,2,72,256]{3,2,1,0:T(8,128)(2,1)S(1)} %sent_sums.1), channel_id=1, source_target_pairs={{0,16},{1,19},{2,18},{3,17},{16,0},{17,3},{18,2},{19,1},{4,20},{5,... | collective-permute-start | bytes 442376 | tf_op jit(solution)/shard_map/ppermute | solution.py:281

commit v6 on v5

--- a/solution.py
+++ b/solution.py
@@ -11,7 +11,8 @@
 FEATS = 256
 EXTRA = 8
 BLOCK_ROWS = LIVE + EXTRA
-EARLY = 48
+EARLY = 56
+TAIL = 4
 LATE = LIVE - EARLY
 NEAR = LIVE + EARLY
 AXES = ("zh", "zl", "yl", "x", "yh", "c")
@@ -70,7 +71,8 @@
 
 
 def join(block, early):
-    return jnp.concatenate([block[:LIVE], early[:EARLY], block[LIVE:] + early[EARLY:]], axis=0)
+    tail = (block[LIVE:] + early[EARLY:])[:TAIL]
+    return jnp.concatenate([block[:LIVE], early[:EARLY], tail], axis=0)
 
 
 def power_below(value):
@@ -113,7 +115,7 @@
                     value = restore(ref[first : first + 128, :])
                     packed_ref[yl, zl, tile * 128 : (tile + 1) * 128, side * 128 : (side + 1) * 128] = value
             for x in range(4):
-                store = pltpu.make_async_copy(packed_ref.at[yl, zl], out_hbm.at[4 * yl + x, zl], out_sems.at[zl, yl, x])
+                store = pltpu.make_async_copy(packed_ref.at[yl, zl], out_hbm.at[2 * x + yl, zl], out_sems.at[zl, yl, x])
                 store.start()
                 stores.append(store)
     for store in stores:
@@ -144,7 +146,7 @@
 
 
 def fetch(w_hbm, w_ref, sems, first):
-    loads = [pltpu.make_async_copy(w_hbm.at[first + x], w_ref.at[x], sems.at[x]) for x in range(4)]
+    loads = [pltpu.make_async_copy(w_hbm.at[2 * x + first], w_ref.at[x], sems.at[x]) for x in range(4)]
     for load in loads:
         load.start()
     return loads
@@ -164,7 +166,7 @@
 
 def sent_kernel(place_ref, own_a_ref, other_a_ref, own_late_ref, other_late_ref, w_hbm, sent_ref, w_ref, sems):
     yl, yh, c = place_ref[0], place_ref[1], place_ref[2]
-    loads = fetch(w_hbm, w_ref, sems, 4 * (1 - yl))
+    loads = fetch(w_hbm, w_ref, sems, 1 - yl)
     index = lax.broadcasted_iota(jnp.int32, (EXTRA, ROWS), 0)
     for i, a_ref in enumerate((own_a_ref, other_a_ref)):
         for flip_h, square in enumerate(square_rows(a_ref)):
@@ -184,7 +186,7 @@
     place_ref, own_a_ref, other_a_ref, own_late_ref, other_late_ref, w_hbm,
     own_ref, square_ref, table_ref, w_ref, sems,
 ):
-    loads = fetch(w_hbm, w_ref, sems, 4 * place_ref[0])
+    loads = fetch(w_hbm, w_ref, sems, place_ref[0])
     total = multiply((own_a_ref, other_a_ref, own_late_ref, other_late_ref), w_ref, loads)
     for i, a_ref in enumerate((own_a_ref, other_a_ref)):
         lives = a_ref[0, NEAR:, :].astype(F32)
@@ -247,7 +249,7 @@
 
 def partner_groups():
     return [
-        [((yl * 4 + x) * 2 + (h ^ (yl & c))) * 2 + c for yl in range(2) for x in range(4)]
+        [((yl * 4 + x) * 2 + (h ^ (yl & c))) * 2 + c for x in range(4) for yl in range(2)]
         for h in range(2)
         for c in range(2)
     ]

time: 84.4 us -> 84.4 us (level)
  waiting for transfers between devices: 4.44 us -> 2.53 us
  local copies, waits for them, and re-layouts: 0.02 us -> 0.94 us
    ppermute x1, waiting for transfers between devices: 1.84 us -> 0.01 us  [shards(): lax.ppermute(late, ('yh', 'c'), [(0, 3), (1, 2), (2, 1), (3, 0)])]
  transfers between devices with their start and end apart: 6 -> 6, of which waited for: 2 -> 1; matrix products, arithmetic and copies ran while one was open for 0% -> 1% of each run, Pallas kernels for 9% -> 9%
where the time goes in v6:
time: 84.4 us; the launch traced here: 83.5 us
  blocking collectives  37.6 us (45%)
  starting transfers between devices  28.7 us (34%)
  Pallas kernels  13.4 us (16%)
  waiting for transfers between devices  2.53 us (3%)
  local copies, waits for them, and re-layouts  0.94 us (1%)
    all_gather x1, blocking collectives, shards(): lax.all_gather(join(block, early), ('zh', 'zl'), axis=0, tiled=False)  37.6 us
    ppermute x1, starting transfers between devices, shards(): other_a = lax.ppermute(own_a, 'c', swap)  7.29 us
    pallas_call x2, Pallas kernels, partial(): pl.pallas_call(kernel, in_specs=[pl.BlockSpec(memory_space=pltpu.SMEM)] +...  5.66 us
    ppermute x1, starting transfers between devices, shards(): early = lax.ppermute(early, 'yh', swap)  5.64 us
    all_to_all x1, starting transfers between devices, shards(): lax.all_to_all(weights, ('yl', 'x', 'yh', 'c'), 0, 0, axis_index_groups=p...  4.58 us
    ppermute x1, starting transfers between devices, shards(): other = lax.ppermute(sent, ('yl', 'yh', 'c'), partner_moves())  4.52 us
    pallas_call x1, Pallas kernels, pack(): pl.pallas_call(pack_kernel, in_specs=[pl.BlockSpec(memory_space=pl.ANY)]...  4.48 us
    ppermute x1, starting transfers between devices, shards(): own_late = lax.ppermute(late, 'yh', swap)  3.54 us
  transfers between devices with their start and end apart: 6, of which 1 were waited for; matrix products, arithmetic and copies ran while one was open for 1% of the time, Pallas kernels for 9%

profile of v6, /device:TPU:1, one launch (start us, length us, event | category | flops | bytes accessed | tf_op | source)
XLA Modules:
  0.0 83.5 jit_solution(4117319310070276487)
XLA Ops:
  0.0 1.8 %compact.1 = (bf16[72,256]{1,0:T(8,128)(2,1)}, bf16[64,256]{1,0:T(8,128)(2,1)}) custom-call(f32[128,256]{1,0:T(8,128)} %stream_ref.1, f32[1,256]{1,0:T(1,128)} %bitcast.7, s32[1,128]{1,0:T(1,128)} %bitcast.8), custom_call_target="tpu_custom_call" | custom-call | tf_op jit(solution)/shard_map/compact/pallas_call | solution.py:63
  1.8 5.6 %collective-permute-start = (bf16[64,256]{1,0:T(8,128)(2,1)}, bf16[64,256]{1,0:T(8,128)(2,1)S(1)}, u32[]{:S(2)}, u32[]{:S(2)}) collective-permute-start(bf16[64,256]{1,0:T(8,128)(2,1)} %get-tuple-element.16), channel_id=1, source_target_pairs={{0,2},{2,0},{1,3},{3,1},{4,6},{6,4},{5,7},{7,5},{8,10},{10,8},{9,1... | collective-permute-start | bytes 98312 | tf_op jit(solution)/shard_map/ppermute | solution.py:271
  7.5 4.5 %pack.1 = bf16[8,4,256,256]{3,2,1,0:T(8,128)(2,1)} custom-call(f32[2048,128]{1,0:T(8,128)} %gate_hbm, f32[2048,128]{1,0:T(8,128)} %up_hbm.1), custom_call_target="tpu_custom_call" | custom-call | tf_op jit(solution)/shard_map/pack/pallas_call | solution.py:126
  11.9 0.0 copy-start
  12.0 0.0 collective-permute-done
  12.0 4.6 %all-to-all-start = ((bf16[8,4,256,256]{3,2,1,0:T(8,128)(2,1)}), bf16[8,4,256,256]{3,2,1,0:T(8,128)(2,1)}, u32[]{:S(2)}, u32[]{:S(2)}) async-start(bf16[8,4,256,256]{3,2,1,0:T(8,128)(2,1)} %pack.1), calls=%async_computation | async-start | bytes 8388608 | tf_op jit(solution)/shard_map/all_to_all | solution.py:275
  16.6 0.0 copy-done
  16.6 37.6 %all-gather.1.own_a_ref = bf16[16,124,256]{2,1,0:T(8,128)(2,1)S(1)} all-gather(bf16[1,124,256]{2,1,0:T(8,128)(2,1)S(1)} %maximum_bitcast_fusion), channel_id=2, replica_groups=mesh['zh'=4,'zl'=4,'yl'=2,'x'=4,'yh'=2,'c'=2] {'zh','zl'}, dimensions={0}, use_global_device_ids=true | all-gather | bytes 1079296 | tf_op jit(solution)/shard_map/all_gather | solution.py:276
  54.3 0.6 copy.6
  54.8 7.3 %collective-permute-start.1 = (bf16[16,124,256]{2,0,1:T(8,128)(2,1)S(1)}, bf16[16,124,256]{2,0,1:T(8,128)(2,1)S(1)}, u32[]{:S(2)}, u32[]{:S(2)}) collective-permute-start(bf16[16,124,256]{2,0,1:T(8,128)(2,1)S(1)} %copy.6), channel_id=1, source_target_pairs={{0,1},{1,0},{2,3},{3,2},{4,5},{5,4},{6,7},{7,6},{8,9},{9,8},{10,11... | collective-permute-start | bytes 3047432 | tf_op jit(solution)/shard_map/ppermute | solution.py:280
  62.1 3.1 %collective-permute-start.3 = (bf16[16,8,256]{2,1,0:T(8,128)(2,1)S(1)}, bf16[16,8,256]{2,1,0:T(8,128)(2,1)S(1)}, u32[]{:S(2)}, u32[]{:S(2)}) collective-permute-start(bf16[16,8,256]{2,1,0:T(8,128)(2,1)S(1)} %slice.26), channel_id=1, source_target_pairs={{0,3},{1,2},{2,1},{3,0},{4,7},{5,6},{6,5},{7,4},{8,11},{9,10},{10,... | collective-permute-start | bytes 196616 | tf_op jit(solution)/shard_map/ppermute | solution.py:279
  65.3 3.5 %collective-permute-start.2 = (bf16[16,8,256]{2,1,0:T(8,128)(2,1)S(1)}, bf16[16,8,256]{2,1,0:T(8,128)(2,1)S(1)}, u32[]{:S(2)}, u32[]{:S(2)}) collective-permute-start(bf16[16,8,256]{2,1,0:T(8,128)(2,1)S(1)} %slice.26), channel_id=1, source_target_pairs={{0,2},{2,0},{1,3},{3,1},{4,6},{6,4},{5,7},{7,5},{8,10},{10,8},{9,1... | collective-permute-start | bytes 196616 | tf_op jit(solution)/shard_map/ppermute | solution.py:278
  68.8 0.1 pad_add_fusion.place_ref
  68.9 0.0 collective-permute-done.1
  68.9 0.3 copy.7.other_a_ref
  69.3 0.0 collective-permute-done.3.other_late_ref
  69.3 2.5 %collective-permute-done.2.own_late_ref = bf16[16,8,256]{2,1,0:T(8,128)(2,1)S(1)} collective-permute-done((bf16[16,8,256]{2,1,0:T(8,128)(2,1)S(1)}, bf16[16,8,256]{2,1,0:T(8,128)(2,1)S(1)}, u32[]{:S(2)}, u32[]{:S(2)}) %collective-permute-start.2) | collective-permute-done | bytes 65568 | tf_op jit(solution)/shard_map/ppermute | solution.py:278
  71.8 0.0 all-to-all-done.w_hbm
  71.8 2.8 %sent_sums.1 = bf16[2,2,72,256]{3,2,1,0:T(8,128)(2,1)S(1)} custom-call(s32[3]{0:T(128)S(1)} %pad_add_fusion.place_ref, bf16[16,124,256]{2,1,0:T(8,128)(2,1)S(1)} %all-gather.1.own_a_ref, bf16[16,124,256]{2,1,0:T(8,128)(2,1)S(1)} %copy.7.other_a_ref, bf16[16,8,256]{2,1,0:T(8,128)(2,1)S(1)} %collective-permute-done.2.own_late_ref, ...), custom_call_target="tpu_custom_call" | custom-call | tf_op jit(solution)/shard_map/sent_sums/pallas_call | solution.py:202
  74.6 4.5 %collective-permute-start.4 = (bf16[2,2,72,256]{3,2,1,0:T(8,128)(2,1)S(1)}, bf16[2,2,72,256]{3,2,1,0:T(8,128)(2,1)S(1)}, u32[]{:S(2)}, u32[]{:S(2)}) collective-permute-start(bf16[2,2,72,256]{3,2,1,0:T(8,128)(2,1)S(1)} %sent_sums.1), channel_id=1, source_target_pairs={{0,16},{1,19},{2,18},{3,17},{16,0},{17,3},{18,2},{19,1},{4,20},{5,... | collective-permute-start | bytes 442376 | tf_op jit(solution)/shard_map/ppermute | solution.py:283
  79.2 2.8 %own_sums.1 = (f32[2,2,64,256]{3,2,1,0:T(8,128)S(1)}, f32[2,2,8,128]{3,2,1,0:T(8,128)S(1)}, bf16[2,2,64,128]{3,2,1,0:T(8,128)(2,1)S(1)}) custom-call(s32[3]{0:T(128)S(1)} %pad_add_fusion.place_ref, bf16[16,124,256]{2,1,0:T(8,128)(2,1)S(1)} %all-gather.1.own_a_ref, bf16[16,124,256]{2,1,0:T(8,128)(2,1)S(1)} %copy.7.other_a_ref, ...), custom_call_target="tpu_custom_call" | custom-call | tf_op jit(solution)/shard_map/own_sums/pallas_call | solution.py:202
  82.0 0.0 collective-permute-done.4.other_ref
  82.0 1.5 %finish.1 = bf16[512,128]{1,0:T(8,128)(2,1)} custom-call(s32[3]{0:T(128)S(1)} %pad_add_fusion.place_ref, f32[2,2,64,256]{3,2,1,0:T(8,128)S(1)} %get-tuple-element.20.own_ref, f32[2,2,8,128]{3,2,1,0:T(8,128)S(1)} %get-tuple-element.21.square_ref, bf16[2,2,64,128]{3,2,1,0:T(8,128)(2,1)S(1)} %get-tuple-element.22.table_ref, ...), custom_call_target="tpu_custom_call" | custom-call | tf_op jit(solution)/shard_map/finish/pallas_call | solution.py:240
  (7 shorter events, 0.0 us)
Async XLA Ops:
  1.8 10.1 %collective-permute-start = (bf16[64,256]{1,0:T(8,128)(2,1)}, bf16[64,256]{1,0:T(8,128)(2,1)S(1)}, u32[]{:S(2)}, u32[]{:S(2)}) collective-permute-start(bf16[64,256]{1,0:T(8,128)(2,1)} %get-tuple-element.16), channel_id=1, source_target_pairs={{0,2},{2,0},{1,3},{3,1},{4,6},{6,4},{5,7},{7,5},{8,10},{10,8},{9,1... | collective-permute-start | bytes 98312 | tf_op jit(solution)/shard_map/ppermute | solution.py:271
  11.9 4.6 %copy-start = (bf16[72,256]{1,0:T(8,128)(2,1)S(1)}, bf16[72,256]{1,0:T(8,128)(2,1)}, u32[]{:S(2)}) copy-start(bf16[72,256]{1,0:T(8,128)(2,1)} %get-tuple-element.15) | copy-start | bytes 110596
  12.0 59.8 %all-to-all-start = ((bf16[8,4,256,256]{3,2,1,0:T(8,128)(2,1)}), bf16[8,4,256,256]{3,2,1,0:T(8,128)(2,1)}, u32[]{:S(2)}, u32[]{:S(2)}) async-start(bf16[8,4,256,256]{3,2,1,0:T(8,128)(2,1)} %pack.1), calls=%async_computation | async-start | bytes 8388608 | tf_op jit(solution)/shard_map/all_to_all | solution.py:275
  54.8 14.1 %collective-permute-start.1 = (bf16[16,124,256]{2,0,1:T(8,128)(2,1)S(1)}, bf16[16,124,256]{2,0,1:T(8,128)(2,1)S(1)}, u32[]{:S(2)}, u32[]{:S(2)}) collective-permute-start(bf16[16,124,256]{2,0,1:T(8,128)(2,1)S(1)} %copy.6), channel_id=1, source_target_pairs={{0,1},{1,0},{2,3},{3,2},{4,5},{5,4},{6,7},{7,6},{8,9},{9,8},{10,11... | collective-permute-start | bytes 3047432 | tf_op jit(solution)/shard_map/ppermute | solution.py:280
  62.1 7.1 %collective-permute-start.3 = (bf16[16,8,256]{2,1,0:T(8,128)(2,1)S(1)}, bf16[16,8,256]{2,1,0:T(8,128)(2,1)S(1)}, u32[]{:S(2)}, u32[]{:S(2)}) collective-permute-start(bf16[16,8,256]{2,1,0:T(8,128)(2,1)S(1)} %slice.26), channel_id=1, source_target_pairs={{0,3},{1,2},{2,1},{3,0},{4,7},{5,6},{6,5},{7,4},{8,11},{9,10},{10,... | collective-permute-start | bytes 196616 | tf_op jit(solution)/shard_map/ppermute | solution.py:279
  65.3 6.5 %collective-permute-start.2 = (bf16[16,8,256]{2,1,0:T(8,128)(2,1)S(1)}, bf16[16,8,256]{2,1,0:T(8,128)(2,1)S(1)}, u32[]{:S(2)}, u32[]{:S(2)}) collective-permute-start(bf16[16,8,256]{2,1,0:T(8,128)(2,1)S(1)} %slice.26), channel_id=1, source_target_pairs={{0,2},{2,0},{1,3},{3,1},{4,6},{6,4},{5,7},{7,5},{8,10},{10,8},{9,1... | collective-permute-start | bytes 196616 | tf_op jit(solution)/shard_map/ppermute | solution.py:278
  74.6 7.4 %collective-permute-start.4 = (bf16[2,2,72,256]{3,2,1,0:T(8,128)(2,1)S(1)}, bf16[2,2,72,256]{3,2,1,0:T(8,128)(2,1)S(1)}, u32[]{:S(2)}, u32[]{:S(2)}) collective-permute-start(bf16[2,2,72,256]{3,2,1,0:T(8,128)(2,1)S(1)} %sent_sums.1), channel_id=1, source_target_pairs={{0,16},{1,19},{2,18},{3,17},{16,0},{17,3},{18,2},{19,1},{4,20},{5,... | collective-permute-start | bytes 442376 | tf_op jit(solution)/shard_map/ppermute | solution.py:283

commit v7 on v6

--- a/solution.py
+++ b/solution.py
@@ -11,8 +11,7 @@
 FEATS = 256
 EXTRA = 8
 BLOCK_ROWS = LIVE + EXTRA
-EARLY = 56
-TAIL = 4
+EARLY = 48
 LATE = LIVE - EARLY
 NEAR = LIVE + EARLY
 AXES = ("zh", "zl", "yl", "x", "yh", "c")
@@ -42,10 +41,17 @@
     return jnp.where((slot == rank) & (live > 0.5), 1.0, 0.0)
 
 
-def compact_kernel(stream_ref, gain_ref, live_ref, block_ref, early_ref):
-    stream = stream_ref[...]
+def compact_kernel(stream_hbm, gain_hbm, live_hbm, block_ref, early_ref, stream_ref, gain_ref, live_ref, sems):
+    pairs = ((live_hbm, live_ref), (gain_hbm, gain_ref), (stream_hbm, stream_ref))
+    loads = [pltpu.make_async_copy(hbm, ref, sems.at[i]) for i, (hbm, ref) in enumerate(pairs)]
+    for load in loads:
+        load.start()
+    loads[0].wait()
     live = live_ref[...].astype(F32)
     table = slot_table(live)
+    loads[1].wait()
+    loads[2].wait()
+    stream = stream_ref[...]
     scaled = (stream * gain_ref[...]).astype(BF)
     rows = jnp.dot(table.astype(BF), scaled, preferred_element_type=F32).astype(BF)
     block_ref[0:LIVE, :] = rows
@@ -62,17 +68,25 @@
 def compact(stream, gain, live):
     return pl.pallas_call(
         compact_kernel,
+        in_specs=[pl.BlockSpec(memory_space=pl.ANY)] * 3,
+        out_specs=[pl.BlockSpec(memory_space=pltpu.VMEM)] * 2,
+        scratch_shapes=[
+            pltpu.VMEM((ROWS, FEATS), F32),
+            pltpu.VMEM((1, FEATS), F32),
+            pltpu.VMEM((1, ROWS), jnp.int32),
+            pltpu.SemaphoreType.DMA((3,)),
+        ],
         out_shape=[
             jax.ShapeDtypeStruct((BLOCK_ROWS, FEATS), BF),
             jax.ShapeDtypeStruct((EARLY + EXTRA, FEATS), BF),
         ],
+        compiler_params=pltpu.CompilerParams(vmem_limit_bytes=62 * 1024 * 1024),
         name="compact",
     )(stream, gain.reshape(1, FEATS), live.reshape(1, ROWS))
 
 
 def join(block, early):
-    tail = (block[LIVE:] + early[EARLY:])[:TAIL]
-    return jnp.concatenate([block[:LIVE], early[:EARLY], tail], axis=0)
+    return jnp.concatenate([block[:LIVE], early[:EARLY], block[LIVE:] + early[EARLY:]], axis=0)
 
 
 def power_below(value):

time: 84.4 us -> 84.4 us (level)
  waiting for transfers between devices: 2.53 us -> 4.44 us
  local copies, waits for them, and re-layouts: 0.94 us -> 0.02 us
    ppermute x1, waiting for transfers between devices: 0.01 us -> 1.74 us  [shards(): lax.ppermute(late, ('yh', 'c'), [(0, 3), (1, 2), (2, 1), (3, 0)])]
  transfers between devices with their start and end apart: 6 -> 6, of which waited for: 1 -> 2; matrix products, arithmetic and copies ran while one was open for 1% -> 0% of each run, Pallas kernels for 9% -> 9%
where the time goes in v7:
time: 84.4 us; the launch traced here: 83.8 us
  blocking collectives  37.1 us (44%)
  starting transfers between devices  28.7 us (34%)
  Pallas kernels  13.3 us (16%)
  waiting for transfers between devices  4.44 us (5%)
    all_gather x1, blocking collectives, shards(): lax.all_gather(join(block, early), ('zh', 'zl'), axis=0, tiled=False)  37.1 us
    ppermute x1, starting transfers between devices, shards(): other_a = lax.ppermute(own_a, 'c', swap)  7.3 us
    ppermute x1, starting transfers between devices, shards(): early = lax.ppermute(early, 'yh', swap)  5.65 us
    pallas_call x2, Pallas kernels, partial(): pl.pallas_call(kernel, in_specs=[pl.BlockSpec(memory_space=pltpu.SMEM)] +...  5.64 us
    all_to_all x1, starting transfers between devices, shards(): lax.all_to_all(weights, ('yl', 'x', 'yh', 'c'), 0, 0, axis_index_groups=p...  4.58 us
    pallas_call x1, Pallas kernels, pack(): pl.pallas_call(pack_kernel, in_specs=[pl.BlockSpec(memory_space=pl.ANY)]...  4.48 us
    ppermute x1, starting transfers between devices, shards(): other = lax.ppermute(sent, ('yl', 'yh', 'c'), partner_moves())  4.46 us
    ppermute x1, starting transfers between devices, shards(): own_late = lax.ppermute(late, 'yh', swap)  3.45 us
  transfers between devices with their start and end apart: 6, of which 2 were waited for; matrix products, arithmetic and copies ran while one was open for 0% of the time, Pallas kernels for 9%

profile of v7, /device:TPU:1, one launch (start us, length us, event | category | flops | bytes accessed | tf_op | source)
XLA Modules:
  0.0 83.8 jit_solution(7356778477608500640)
XLA Ops:
  0.0 1.7 %compact.1 = (bf16[72,256]{1,0:T(8,128)(2,1)}, bf16[56,256]{1,0:T(8,128)(2,1)}) custom-call(f32[128,256]{1,0:T(8,128)} %stream_hbm.1, f32[1,256]{1,0:T(1,128)} %bitcast.10, s32[1,128]{1,0:T(1,128)} %bitcast.11), custom_call_target="tpu_custom_call" | custom-call | tf_op jit(solution)/shard_map/compact/pallas_call | solution.py:69
  1.7 5.7 %collective-permute-start = (bf16[56,256]{1,0:T(8,128)(2,1)}, bf16[56,256]{1,0:T(8,128)(2,1)S(1)}, u32[]{:S(2)}, u32[]{:S(2)}) collective-permute-start(bf16[56,256]{1,0:T(8,128)(2,1)} %get-tuple-element.16), channel_id=1, source_target_pairs={{0,2},{2,0},{1,3},{3,1},{4,6},{6,4},{5,7},{7,5},{8,10},{10,8},{9,1... | collective-permute-start | bytes 86024 | tf_op jit(solution)/shard_map/ppermute | solution.py:285
  7.4 4.5 %pack.1 = bf16[8,4,256,256]{3,2,1,0:T(8,128)(2,1)} custom-call(f32[2048,128]{1,0:T(8,128)} %gate_hbm, f32[2048,128]{1,0:T(8,128)} %up_hbm.1), custom_call_target="tpu_custom_call" | custom-call | tf_op jit(solution)/shard_map/pack/pallas_call | solution.py:140
  11.9 0.0 copy-start
  11.9 0.0 collective-permute-done
  11.9 4.6 %all-to-all-start = ((bf16[8,4,256,256]{3,2,1,0:T(8,128)(2,1)}), bf16[8,4,256,256]{3,2,1,0:T(8,128)(2,1)}, u32[]{:S(2)}, u32[]{:S(2)}) async-start(bf16[8,4,256,256]{3,2,1,0:T(8,128)(2,1)} %pack.1), calls=%async_computation | async-start | bytes 8388608 | tf_op jit(solution)/shard_map/all_to_all | solution.py:289
  16.5 0.0 copy-done
  16.6 37.1 %all-gather = bf16[1920,256]{1,0:T(8,128)(2,1)S(1)} all-gather(bf16[120,256]{1,0:T(8,128)(2,1)S(1)} %pad_maximum_fusion), channel_id=2, replica_groups=mesh['zh'=4,'zl'=4,'yl'=2,'x'=4,'yh'=2,'c'=2] {'zh','zl'}, dimensions={0}, use_global_device_ids=true | all-gather | bytes 1044480 | tf_op jit(solution)/shard_map/all_gather | solution.py:290
  53.6 7.3 %collective-permute-start.1 = (bf16[16,120,256]{2,1,0:T(8,128)(2,1)S(1)}, bf16[16,120,256]{2,1,0:T(8,128)(2,1)S(1)}, u32[]{:S(2)}, u32[]{:S(2)}) collective-permute-start(bf16[16,120,256]{2,1,0:T(8,128)(2,1)S(1)} %bitcast.6), channel_id=1, source_target_pairs={{0,1},{1,0},{2,3},{3,2},{4,5},{5,4},{6,7},{7,6},{8,9},{9,8},{10,11... | collective-permute-start | bytes 2949128 | tf_op jit(solution)/shard_map/ppermute | solution.py:294
  60.9 3.2 %collective-permute-start.3 = (bf16[16,16,256]{2,1,0:T(8,128)(2,1)S(1)}, bf16[16,16,256]{2,1,0:T(8,128)(2,1)S(1)}, u32[]{:S(2)}, u32[]{:S(2)}) collective-permute-start(bf16[16,16,256]{2,1,0:T(8,128)(2,1)S(1)} %slice.20), channel_id=1, source_target_pairs={{0,3},{1,2},{2,1},{3,0},{4,7},{5,6},{6,5},{7,4},{8,11},{9,10},{10,... | collective-permute-start | bytes 393224 | tf_op jit(solution)/shard_map/ppermute | solution.py:293
  64.2 3.4 %collective-permute-start.2 = (bf16[16,16,256]{2,1,0:T(8,128)(2,1)S(1)}, bf16[16,16,256]{2,1,0:T(8,128)(2,1)S(1)}, u32[]{:S(2)}, u32[]{:S(2)}) collective-permute-start(bf16[16,16,256]{2,1,0:T(8,128)(2,1)S(1)} %slice.20), channel_id=1, source_target_pairs={{0,2},{2,0},{1,3},{3,1},{4,6},{6,4},{5,7},{7,5},{8,10},{10,8},{9,1... | collective-permute-start | bytes 393224 | tf_op jit(solution)/shard_map/ppermute | solution.py:292
  67.6 0.1 pad_add_fusion.place_ref
  67.7 1.7 %collective-permute-done.3.other_late_ref = bf16[16,16,256]{2,1,0:T(8,128)(2,1)S(1)} collective-permute-done((bf16[16,16,256]{2,1,0:T(8,128)(2,1)S(1)}, bf16[16,16,256]{2,1,0:T(8,128)(2,1)S(1)}, u32[]{:S(2)}, u32[]{:S(2)}) %collective-permute-start.3) | collective-permute-done | bytes 131104 | tf_op jit(solution)/shard_map/ppermute | solution.py:293
  69.5 2.7 %collective-permute-done.2.own_late_ref = bf16[16,16,256]{2,1,0:T(8,128)(2,1)S(1)} collective-permute-done((bf16[16,16,256]{2,1,0:T(8,128)(2,1)S(1)}, bf16[16,16,256]{2,1,0:T(8,128)(2,1)S(1)}, u32[]{:S(2)}, u32[]{:S(2)}) %collective-permute-start.2) | collective-permute-done | bytes 131104 | tf_op jit(solution)/shard_map/ppermute | solution.py:292
  72.2 0.0 collective-permute-done.1.other_a_ref
  72.2 0.0 all-to-all-done.w_hbm
  72.2 2.8 %sent_sums.1 = bf16[2,2,72,256]{3,2,1,0:T(8,128)(2,1)S(1)} custom-call(s32[3]{0:T(128)S(1)} %pad_add_fusion.place_ref, bf16[16,120,256]{2,1,0:T(8,128)(2,1)S(1)} %bitcast.8, bf16[16,120,256]{2,1,0:T(8,128)(2,1)S(1)} %collective-permute-done.1.other_a_ref, bf16[16,16,256]{2,1,0:T(8,128)(2,1)S(1)} %collective-permute-done.2.own_late_ref, ...), custom_call_target="tpu_custom_call" | custom-call | tf_op jit(solution)/shard_map/sent_sums/pallas_call | solution.py:216
  75.0 4.5 %collective-permute-start.4 = (bf16[2,2,72,256]{3,2,1,0:T(8,128)(2,1)S(1)}, bf16[2,2,72,256]{3,2,1,0:T(8,128)(2,1)S(1)}, u32[]{:S(2)}, u32[]{:S(2)}) collective-permute-start(bf16[2,2,72,256]{3,2,1,0:T(8,128)(2,1)S(1)} %sent_sums.1), channel_id=1, source_target_pairs={{0,16},{1,19},{2,18},{3,17},{16,0},{17,3},{18,2},{19,1},{4,20},{5,... | collective-permute-start | bytes 442376 | tf_op jit(solution)/shard_map/ppermute | solution.py:297
  79.4 2.8 %own_sums.1 = (f32[2,2,64,256]{3,2,1,0:T(8,128)S(1)}, f32[2,2,8,128]{3,2,1,0:T(8,128)S(1)}, bf16[2,2,64,128]{3,2,1,0:T(8,128)(2,1)S(1)}) custom-call(s32[3]{0:T(128)S(1)} %pad_add_fusion.place_ref, bf16[16,120,256]{2,1,0:T(8,128)(2,1)S(1)} %bitcast.9, bf16[16,120,256]{2,1,0:T(8,128)(2,1)S(1)} %collective-permute-done.1.other_a_ref, ...), custom_call_target="tpu_custom_call" | custom-call | tf_op jit(solution)/shard_map/own_sums/pallas_call | solution.py:216
  82.3 0.0 collective-permute-done.4.other_ref
  82.3 1.5 %finish.1 = bf16[512,128]{1,0:T(8,128)(2,1)} custom-call(s32[3]{0:T(128)S(1)} %pad_add_fusion.place_ref, f32[2,2,64,256]{3,2,1,0:T(8,128)S(1)} %get-tuple-element.20.own_ref, f32[2,2,8,128]{3,2,1,0:T(8,128)S(1)} %get-tuple-element.21.square_ref, bf16[2,2,64,128]{3,2,1,0:T(8,128)(2,1)S(1)} %get-tuple-element.22.table_ref, ...), custom_call_target="tpu_custom_call" | custom-call | tf_op jit(solution)/shard_map/finish/pallas_call | solution.py:254
  (5 shorter events, 0.0 us)
Async XLA Ops:
  1.7 10.2 %collective-permute-start = (bf16[56,256]{1,0:T(8,128)(2,1)}, bf16[56,256]{1,0:T(8,128)(2,1)S(1)}, u32[]{:S(2)}, u32[]{:S(2)}) collective-permute-start(bf16[56,256]{1,0:T(8,128)(2,1)} %get-tuple-element.16), channel_id=1, source_target_pairs={{0,2},{2,0},{1,3},{3,1},{4,6},{6,4},{5,7},{7,5},{8,10},{10,8},{9,1... | collective-permute-start | bytes 86024 | tf_op jit(solution)/shard_map/ppermute | solution.py:285
  11.9 4.6 %copy-start = (bf16[72,256]{1,0:T(8,128)(2,1)S(1)}, bf16[72,256]{1,0:T(8,128)(2,1)}, u32[]{:S(2)}) copy-start(bf16[72,256]{1,0:T(8,128)(2,1)} %get-tuple-element.15) | copy-start | bytes 110596
  11.9 60.3 %all-to-all-start = ((bf16[8,4,256,256]{3,2,1,0:T(8,128)(2,1)}), bf16[8,4,256,256]{3,2,1,0:T(8,128)(2,1)}, u32[]{:S(2)}, u32[]{:S(2)}) async-start(bf16[8,4,256,256]{3,2,1,0:T(8,128)(2,1)} %pack.1), calls=%async_computation | async-start | bytes 8388608 | tf_op jit(solution)/shard_map/all_to_all | solution.py:289
  53.6 18.5 %collective-permute-start.1 = (bf16[16,120,256]{2,1,0:T(8,128)(2,1)S(1)}, bf16[16,120,256]{2,1,0:T(8,128)(2,1)S(1)}, u32[]{:S(2)}, u32[]{:S(2)}) collective-permute-start(bf16[16,120,256]{2,1,0:T(8,128)(2,1)S(1)} %bitcast.6), channel_id=1, source_target_pairs={{0,1},{1,0},{2,3},{3,2},{4,5},{5,4},{6,7},{7,6},{8,9},{9,8},{10,11... | collective-permute-start | bytes 2949128 | tf_op jit(solution)/shard_map/ppermute | solution.py:294
  60.9 8.5 %collective-permute-start.3 = (bf16[16,16,256]{2,1,0:T(8,128)(2,1)S(1)}, bf16[16,16,256]{2,1,0:T(8,128)(2,1)S(1)}, u32[]{:S(2)}, u32[]{:S(2)}) collective-permute-start(bf16[16,16,256]{2,1,0:T(8,128)(2,1)S(1)} %slice.20), channel_id=1, source_target_pairs={{0,3},{1,2},{2,1},{3,0},{4,7},{5,6},{6,5},{7,4},{8,11},{9,10},{10,... | collective-permute-start | bytes 393224 | tf_op jit(solution)/shard_map/ppermute | solution.py:293
  64.2 8.0 %collective-permute-start.2 = (bf16[16,16,256]{2,1,0:T(8,128)(2,1)S(1)}, bf16[16,16,256]{2,1,0:T(8,128)(2,1)S(1)}, u32[]{:S(2)}, u32[]{:S(2)}) collective-permute-start(bf16[16,16,256]{2,1,0:T(8,128)(2,1)S(1)} %slice.20), channel_id=1, source_target_pairs={{0,2},{2,0},{1,3},{3,1},{4,6},{6,4},{5,7},{7,5},{8,10},{10,8},{9,1... | collective-permute-start | bytes 393224 | tf_op jit(solution)/shard_map/ppermute | solution.py:292
  75.0 7.3 %collective-permute-start.4 = (bf16[2,2,72,256]{3,2,1,0:T(8,128)(2,1)S(1)}, bf16[2,2,72,256]{3,2,1,0:T(8,128)(2,1)S(1)}, u32[]{:S(2)}, u32[]{:S(2)}) collective-permute-start(bf16[2,2,72,256]{3,2,1,0:T(8,128)(2,1)S(1)} %sent_sums.1), channel_id=1, source_target_pairs={{0,16},{1,19},{2,18},{3,17},{16,0},{17,3},{18,2},{19,1},{4,20},{5,... | collective-permute-start | bytes 442376 | tf_op jit(solution)/shard_map/ppermute | solution.py:297
